TPU v7x, 512 devices: a whole 4x4x16 slice. The times are simulated.
512 devices in a mesh: grp: 8 (over y, core), tile: 64 (over z, x).
Axes of the slice: x: 4, y: 4, z: 16, core: 2. Of those that a mesh axis runs over, the one named last changes fastest.
Arguments:
- spectrum: float32 [36, 36, 131072], P(None, None, ('grp', 'tile')), may hold values from 0 to 2
- courant: float32 [36], replicated, may hold values from 0.15 to 0.7
- decay: float32 [36], replicated, may hold values from 0.05 to 0.5
- land: int32 [1024, 128], P('tile', 'grp'), may hold values 0 or 1
- ice_rows: float32 [3, 131072], P(None, ('grp', 'tile')), may hold values from 0 to 1
- ice_route: int32 [2, 131072], P(None, ('grp', 'tile')), may hold values from 0 to 63, as said below
- wave_source: int32 [2, 1024, 128], P(None, 'tile', 'grp'), may hold values from 0 to 63, as said below
Outputs:
- spectrum_out: float32 [36, 36, 131072], P(None, None, ('grp', 'tile'))
- coupling: float32 [4, 131072], P(None, ('grp', 'tile'))
Inputs may be any that keep to these rules, and one draw needn't show every extreme that they name: `ice_route`: row 0 is a tile index, row 1 a slot. Within a group, the rows of ice device t with tile index d take slots 0 to n-1 once each, where n is at most 6, equals 6 for exactly one d of every t and 2 for exactly one other. `wave_source`: row 0 is an ice device index within the group, row 1 a slot; the cells of wave device (g, d) hold exactly the pairs (t, s) of the rows of group g that ice_route sends to d, each once.
All inputs are finite; a program needn't handle non-finite values. No bound on the sum of `land` on one device may be relied on, other than what follows from the above.
Results may differ from a plain program's by a relative error of at most 0.00014.
Values sent between devices are 32-bit elements; how exact they have to be, the bound alone decides.
A program may use at most 128 MiB of HBM per device.

v0:
```python
import jax
import jax.numpy as jnp
from jax import lax
from jax.sharding import PartitionSpec as P


def with_halo(x, sides, width):
    for axis, dim in sides:
        size, length = (lax.axis_size(axis), x.shape[dim])
        up = [(i, (i + 1) % size) for i in range(size - 1)]
        down = [(j, i) for i, j in up]
        last = lax.slice_in_dim(x, length - width, length, axis=dim)
        initial = lax.slice_in_dim(x, 0, width, axis=dim)
        before = lax.ppermute(last, axis, up)
        after = lax.ppermute(initial, axis, down)
        x = jnp.concatenate([before, x, after], axis=dim)
    return x


def advect(padded, east, north):
    inner = padded[:, :, 1:-1, 1:-1]
    west_cell = padded[:, :, :-2, 1:-1]
    east_cell = padded[:, :, 2:, 1:-1]
    south_cell = padded[:, :, 1:-1, :-2]
    north_cell = padded[:, :, 1:-1, 2:]
    return (
        inner
        - jnp.maximum(east, 0.0) * (inner - west_cell)
        - jnp.maximum(-east, 0.0) * (inner - east_cell)
        - jnp.maximum(north, 0.0) * (inner - south_cell)
        - jnp.maximum(-north, 0.0) * (inner - north_cell)
    )


def body(spectrum, courant, decay, land, ice_rows, ice_route, wave_source):
    tile_count = lax.axis_size("tile")
    width_x, width_y = land.shape
    dirs, freqs = (spectrum.shape[0], spectrum.shape[1])
    cell_count = width_x * width_y
    base_rows = cell_count // tile_count
    capacity = base_rows + base_rows // 2
    send_slot = ice_route[0] * capacity + ice_route[1]
    outgoing = jnp.zeros((3, tile_count * capacity), jnp.float32).at[:, send_slot].set(ice_rows)
    received = lax.all_to_all(outgoing, "tile", split_axis=1, concat_axis=1, tiled=True)
    source_slot = (wave_source[0] * capacity + wave_source[1]).reshape(-1)
    field = received[:, source_slot].reshape(3, width_x, width_y)
    concentration, thickness, floe = (field[0], field[1], field[2])
    freq = jnp.arange(freqs).astype(jnp.float32)
    wavelen = jnp.exp(-0.2 * freq)[:, None, None]
    rate = (
        decay[:, None, None]
        * concentration[None]
        * (thickness[None] + wavelen / (wavelen + floe[None]))
    )
    factor = land.astype(jnp.float32)[None] * jnp.exp(-rate)
    angle = 2.0 * jnp.pi * (jnp.arange(dirs).astype(jnp.float32) + 0.5) / dirs
    cosine = jnp.cos(angle)
    sine = jnp.sin(angle)
    east = (cosine[:, None] * courant[None, :])[:, :, None, None]
    north = (sine[:, None] * courant[None, :])[:, :, None, None]
    grid_spectrum = spectrum.reshape(dirs, freqs, width_x, width_y)
    energy = grid_spectrum
    for substep in range(2):
        padded = with_halo(energy, (("grp", 3), ("tile", 2)), 1)
        energy = factor[None] * advect(padded, east, north)
    zonal = jnp.einsum("tkxy,t->kxy", energy, cosine, precision=lax.Precision.HIGHEST)
    meridional = jnp.einsum("tkxy,t->kxy", energy, sine, precision=lax.Precision.HIGHEST)
    raw_weight = jnp.exp(0.1 * freq)
    weights = 3.0 * raw_weight / jnp.sum(raw_weight)
    stokes_x = jnp.einsum("kxy,k->xy", zonal, weights, precision=lax.Precision.HIGHEST)
    stokes_y = jnp.einsum("kxy,k->xy", meridional, weights, precision=lax.Precision.HIGHEST)
    stress_x = jnp.sum(rate * zonal, 0) * (4.0 / freqs)
    stress_y = jnp.sum(rate * meridional, 0) * (4.0 / freqs)
    values = jnp.stack([stokes_x, stokes_y, stress_x, stress_y]).reshape(4, cell_count)
    returning = jnp.zeros((4, tile_count * capacity), jnp.float32).at[:, source_slot].set(values)
    arrived = lax.all_to_all(returning, "tile", split_axis=1, concat_axis=1, tiled=True)
    coupling = arrived[:, send_slot]
    return (energy.reshape(dirs, freqs, cell_count), coupling)


def solution(mesh):
    in_specs = (
        P(None, None, ("grp", "tile")),
        P(),
        P(),
        P("tile", "grp"),
        P(None, ("grp", "tile")),
        P(None, ("grp", "tile")),
        P(None, "tile", "grp"),
    )
    out_specs = (P(None, None, ("grp", "tile")), P(None, ("grp", "tile")))
    return jax.shard_map(body, mesh=mesh, in_specs=in_specs, out_specs=out_specs, check_vma=False)
```

profile of v0, /device:TPU:8, one launch (start us, length us, event | category | flops | bytes accessed | tf_op | source)
XLA Modules:
  0.0 187.6 jit_solution(5194409664048859933)
XLA Ops:
  0.7 0.8 compare_select_fusion.1
  1.4 0.8 copy.20
  2.2 1.2 scatter_custom_fusion
  3.5 0.2 all_to_all.16
  3.7 0.7 copy.22
  4.4 18.6 %all-to-all-start = ((f32[3,64,6]{2,0,1:T(4,128)}), f32[3,64,6]{2,0,1:T(4,128)S(1)}, u32[]{:S(2)}, u32[]{:S(2)}) async-start(f32[3,64,6]{2,0,1:T(4,128)} %copy.22), calls=%async_computation | async-start | bytes 262144 | tf_op jit(solution)/shard_map/all_to_all | solution.py:44
  23.0 4.0 %copy.25 = f32[36,36,256]{1,2,0:T(8,128)} copy(f32[36,36,256]{2,1,0:T(8,128)} %param.7) | data formatting | bytes 2654208 | tf_op args[0]
  27.0 2.9 %fusion.54 = (f32[36,36,16,1]{1,3,2,0:T(1,128)S(1)}, f32[36,36,16,1]{1,3,2,0:T(1,128)S(1)}) fusion(f32[36,36,16,16]{1,3,2,0:T(8,128)} %bitcast.39), kind=kLoop, calls=%fused_computation.101 | loop fusion | bytes 331776 | tf_op jit(solution)/shard_map/slice | solution.py:12
  29.9 1.9 %collective-permute-start = (f32[36,36,16,1]{1,3,2,0:T(1,128)S(1)}, f32[36,36,16,1]{1,3,2,0:T(1,128)S(1)}, u32[]{:S(2)}, u32[]{:S(2)}) collective-permute-start(f32[36,36,16,1]{1,3,2,0:T(1,128)S(1)} %get-tuple-element.19), channel_id=1, source_target_pairs={{0,64},{64,128},{128,192},{192,256},{256,320},{320,384},{384,448},... | collective-permute-start | bytes 248840 | tf_op jit(solution)/shard_map/ppermute | solution.py:14
  31.8 3.6 %collective-permute-start.1 = (f32[36,36,16,1]{1,3,2,0:T(1,128)S(1)}, f32[36,36,16,1]{1,3,2,0:T(1,128)S(1)}, u32[]{:S(2)}, u32[]{:S(2)}) collective-permute-start(f32[36,36,16,1]{1,3,2,0:T(1,128)S(1)} %get-tuple-element.20), channel_id=1, source_target_pairs={{64,0},{128,64},{192,128},{256,192},{320,256},{384,320},{448,384},... | collective-permute-start | bytes 248840 | tf_op jit(solution)/shard_map/ppermute | solution.py:15
  35.8 4.9 %all-to-all-done = f32[3,64,6]{2,0,1:T(4,128)S(1)} async-done(((f32[3,64,6]{2,0,1:T(4,128)}), f32[3,64,6]{2,0,1:T(4,128)S(1)}, u32[]{:S(2)}, u32[]{:S(2)}) %all-to-all-start) | async-done | bytes 4640 | tf_op jit(solution)/shard_map/all_to_all | solution.py:44
  40.9 0.1 copy.24
  41.0 0.7 gather_fusion
  41.7 0.3 slice_reduce_fusion.2
  42.3 1.4 pad_maximum_fusion.21
  43.6 2.5 %collective-permute-start.2 = (f32[36,36,1,18]{1,3,2,0:T(8,128)S(1)}, f32[36,36,1,18]{1,3,2,0:T(8,128)S(1)}, u32[]{:S(2)}, u32[]{:S(2)}) collective-permute-start(f32[36,36,1,18]{1,3,2,0:T(8,128)S(1)} %get-tuple-element.15), channel_id=1, source_target_pairs={{0,1},{1,2},{2,3},{3,4},{4,5},{5,6},{6,7},{7,8},{8,9},{9,10},{10,1... | collective-permute-start | bytes 279944 | tf_op jit(solution)/shard_map/ppermute | solution.py:14
  46.2 1.3 collective-permute-start.3
  47.5 0.2 exponential_multiply_fusion
  47.7 8.1 %collective-permute-done.2 = f32[36,36,1,18]{1,3,2,0:T(8,128)S(1)} collective-permute-done((f32[36,36,1,18]{1,3,2,0:T(8,128)S(1)}, f32[36,36,1,18]{1,3,2,0:T(8,128)S(1)}, u32[]{:S(2)}, u32[]{:S(2)}) %collective-permute-start.2) | collective-permute-done | bytes 93344 | tf_op jit(solution)/shard_map/ppermute | solution.py:14
  55.8 4.1 %collective-permute-done.3 = f32[36,36,1,18]{1,3,2,0:T(8,128)S(1)} collective-permute-done((f32[36,36,1,18]{1,3,2,0:T(8,128)S(1)}, f32[36,36,1,18]{1,3,2,0:T(8,128)S(1)}, u32[]{:S(2)}, u32[]{:S(2)}) %collective-permute-start.3) | collective-permute-done | bytes 93344 | tf_op jit(solution)/shard_map/ppermute | solution.py:15
  60.0 5.3 %fusion.16 = f32[36,36,16,16]{1,3,2,0:T(8,128)S(1)} fusion(f32[36,36,16,16]{1,3,2,0:T(8,128)S(1)} %bitcast.41, f32[36,36,16,1]{1,3,2,0:T(1,128)S(1)} %collective-permute-done.1, f32[36,36,16,1]{1,3,2,0:T(1,128)S(1)} %collective-permute-done, f32[36,36,1,18]{1,3,2,0:T(8,128)S(1)} %collective-permute-done.3, f32[36,36,1,18]{1,3,2,0:T(8,128)S(1)} %collective-permute-done.2, ...), kind=kLoop, calls=%fused_computation.29 | loop fusion | flops 6967296 | bytes 3064320 | tf_op jit(solution)/shard_map/mul | solution.py:65
  65.2 0.4 fusion.53
  65.7 1.9 %collective-permute-start.4 = (f32[36,36,16,1]{1,3,2,0:T(1,128)S(1)}, f32[36,36,16,1]{1,3,2,0:T(1,128)S(1)}, u32[]{:S(2)}, u32[]{:S(2)}) collective-permute-start(f32[36,36,16,1]{1,3,2,0:T(1,128)S(1)} %get-tuple-element.17), channel_id=1, source_target_pairs={{0,64},{64,128},{128,192},{192,256},{256,320},{320,384},{384,448},... | collective-permute-start | bytes 248840 | tf_op jit(solution)/shard_map/ppermute | solution.py:14
  67.6 3.6 %collective-permute-start.5 = (f32[36,36,16,1]{1,3,2,0:T(1,128)S(1)}, f32[36,36,16,1]{1,3,2,0:T(1,128)S(1)}, u32[]{:S(2)}, u32[]{:S(2)}) collective-permute-start(f32[36,36,16,1]{1,3,2,0:T(1,128)S(1)} %get-tuple-element.18), channel_id=1, source_target_pairs={{64,0},{128,64},{192,128},{256,192},{320,256},{384,320},{448,384},... | collective-permute-start | bytes 248840 | tf_op jit(solution)/shard_map/ppermute | solution.py:15
  71.2 2.5 %collective-permute-done.4 = f32[36,36,16,1]{1,3,2,0:T(1,128)S(1)} collective-permute-done((f32[36,36,16,1]{1,3,2,0:T(1,128)S(1)}, f32[36,36,16,1]{1,3,2,0:T(1,128)S(1)}, u32[]{:S(2)}, u32[]{:S(2)}) %collective-permute-start.4) | collective-permute-done | bytes 82976 | tf_op jit(solution)/shard_map/ppermute | solution.py:14
  73.7 1.8 collective-permute-done.5
  75.5 0.2 pad_maximum_fusion.18
  75.6 3.4 %collective-permute-start.6 = (f32[36,36,1,18]{1,3,2,0:T(8,128)S(1)}, f32[36,36,1,18]{1,3,2,0:T(8,128)S(1)}, u32[]{:S(2)}, u32[]{:S(2)}) collective-permute-start(f32[36,36,1,18]{1,3,2,0:T(8,128)S(1)} %get-tuple-element.13), channel_id=1, source_target_pairs={{0,1},{1,2},{2,3},{3,4},{4,5},{5,6},{6,7},{7,8},{8,9},{9,10},{10,1... | collective-permute-start | bytes 279944 | tf_op jit(solution)/shard_map/ppermute | solution.py:14
  79.0 1.3 collective-permute-start.7
  80.3 0.6 fusion.42
  80.9 8.1 %collective-permute-done.6 = f32[36,36,1,18]{1,3,2,0:T(8,128)S(1)} collective-permute-done((f32[36,36,1,18]{1,3,2,0:T(8,128)S(1)}, f32[36,36,1,18]{1,3,2,0:T(8,128)S(1)}, u32[]{:S(2)}, u32[]{:S(2)}) %collective-permute-start.6) | collective-permute-done | bytes 93344 | tf_op jit(solution)/shard_map/ppermute | solution.py:14
  89.0 4.6 %collective-permute-done.7 = f32[36,36,1,18]{1,3,2,0:T(8,128)S(1)} collective-permute-done((f32[36,36,1,18]{1,3,2,0:T(8,128)S(1)}, f32[36,36,1,18]{1,3,2,0:T(8,128)S(1)}, u32[]{:S(2)}, u32[]{:S(2)}) %collective-permute-start.7) | collective-permute-done | bytes 93344 | tf_op jit(solution)/shard_map/ppermute | solution.py:15
  93.6 6.6 %fusion.3 = f32[36,36,16,16]{1,3,2,0:T(8,128)} fusion(f32[36,36,16,16]{1,3,2,0:T(8,128)S(1)} %fusion.16, f32[36,36,16,1]{1,3,2,0:T(1,128)S(1)} %collective-permute-done.5, f32[36,36,16,1]{1,3,2,0:T(1,128)S(1)} %collective-permute-done.4, f32[36,36,1,18]{1,3,2,0:T(8,128)S(1)} %collective-permute-done.7, f32[36,36,1,18]{1,3,2,0:T(8,128)S(1)} %collective-permute-done.6, ...), kind=kLoop, calls=%fused_computation.8 | loop fusion | flops 6967296 | bytes 3064320 | tf_op jit(solution)/shard_map/mul | solution.py:65
  100.2 6.5 %copy.33 = f32[36,36,16,16]{0,1,3,2:T(8,128)} copy(f32[36,36,16,16]{1,3,2,0:T(8,128)} %fusion.3) | data formatting | bytes 2654208 | tf_op jit(solution)/shard_map/mul | solution.py:65
  106.7 19.7 %fusion.34 = f32[1,36,16,16]{1,0,3,2:T(1,128)S(1)} fusion(f32[36,36,16,16]{0,1,3,2:T(8,128)} %copy.33), kind=kOutput, calls=%fused_computation.79 | convolution fusion | flops 3981420 | bytes 1363968 | tf_op jit(solution)/shard_map/tkxy,t->kxy/dot_general | solution.py:66
  126.5 17.3 %fusion.32 = f32[1,36,16,16]{1,0,3,2:T(1,128)S(1)} fusion(f32[36,36,16,16]{0,1,3,2:T(8,128)S(1)} %copy-done), kind=kOutput, calls=%fused_computation.77 | convolution fusion | flops 3981420 | bytes 1363968 | tf_op jit(solution)/shard_map/tkxy,t->kxy/dot_general | solution.py:67
  143.8 0.3 multiply_reduce_fusion.1
  144.1 1.7 fusion.38
  145.7 1.7 fusion.36
  147.9 1.2 scatter_custom_fusion.1
  149.2 0.2 all_to_all.19
  149.4 0.7 copy.28
  150.2 17.0 %all-to-all-start.1 = ((f32[4,64,6]{2,0,1:T(4,128)}), f32[4,64,6]{2,0,1:T(4,128)S(1)}, u32[]{:S(2)}, u32[]{:S(2)}) async-start(f32[4,64,6]{2,0,1:T(4,128)} %copy.28), calls=%async_computation.1 | async-start | bytes 262144 | tf_op jit(solution)/shard_map/all_to_all | solution.py:76
  167.2 3.9 %copy.31 = f32[36,36,256]{2,1,0:T(8,128)} copy(f32[36,36,256]{1,2,0:T(8,128)} %bitcast.42) | data formatting | bytes 2654208
  171.1 14.8 %all-to-all-done.1 = f32[4,64,6]{2,0,1:T(4,128)S(1)} async-done(((f32[4,64,6]{2,0,1:T(4,128)}), f32[4,64,6]{2,0,1:T(4,128)S(1)}, u32[]{:S(2)}, u32[]{:S(2)}) %all-to-all-start.1) | async-done | bytes 6176 | tf_op jit(solution)/shard_map/all_to_all | solution.py:76
  186.1 0.1 copy.30
  186.2 0.7 gather_fusion.1
  187.0 0.7 copy.32
  (40 shorter events, 1.5 us)
Async XLA Ops:
  0.6 34.9 %copy-start.2 = (s32[2,16,16]{2,1,0:T(8,128)S(1)}, s32[2,16,16]{2,1,0:T(8,128)}, u32[]{:S(2)}) copy-start(s32[2,16,16]{2,1,0:T(8,128)} %param.13) | copy-start | bytes 6148
  0.6 35.0 %copy-start.5 = (f32[36]{0:T(128)S(1)}, f32[36]{0:T(128)}, u32[]{:S(2)}) copy-start(f32[36]{0:T(128)} %param.8) | copy-start | bytes 436
  0.7 35.1 %copy-start.3 = (s32[16,16]{1,0:T(8,128)S(1)}, s32[16,16]{1,0:T(8,128)}, u32[]{:S(2)}) copy-start(s32[16,16]{1,0:T(8,128)} %param.10) | copy-start | bytes 3076
  4.4 36.2 %all-to-all-start = ((f32[3,64,6]{2,0,1:T(4,128)}), f32[3,64,6]{2,0,1:T(4,128)S(1)}, u32[]{:S(2)}, u32[]{:S(2)}) async-start(f32[3,64,6]{2,0,1:T(4,128)} %copy.22), calls=%async_computation | async-start | bytes 262144 | tf_op jit(solution)/shard_map/all_to_all | solution.py:44
  27.0 20.5 %copy-start.4 = (f32[36]{0:T(128)S(1)}, f32[36]{0:T(128)}, u32[]{:S(2)}) copy-start(f32[36]{0:T(128)} %param.9) | copy-start | bytes 436
  29.9 12.4 %collective-permute-start = (f32[36,36,16,1]{1,3,2,0:T(1,128)S(1)}, f32[36,36,16,1]{1,3,2,0:T(1,128)S(1)}, u32[]{:S(2)}, u32[]{:S(2)}) collective-permute-start(f32[36,36,16,1]{1,3,2,0:T(1,128)S(1)} %get-tuple-element.19), channel_id=1, source_target_pairs={{0,64},{64,128},{128,192},{192,256},{256,320},{320,384},{384,448},... | collective-permute-start | bytes 248840 | tf_op jit(solution)/shard_map/ppermute | solution.py:14
  31.8 10.4 %collective-permute-start.1 = (f32[36,36,16,1]{1,3,2,0:T(1,128)S(1)}, f32[36,36,16,1]{1,3,2,0:T(1,128)S(1)}, u32[]{:S(2)}, u32[]{:S(2)}) collective-permute-start(f32[36,36,16,1]{1,3,2,0:T(1,128)S(1)} %get-tuple-element.20), channel_id=1, source_target_pairs={{64,0},{128,64},{192,128},{256,192},{320,256},{384,320},{448,384},... | collective-permute-start | bytes 248840 | tf_op jit(solution)/shard_map/ppermute | solution.py:15
  42.2 17.7 %copy-start.1 = (f32[36,36,256]{1,2,0:T(8,128)S(1)}, f32[36,36,256]{1,2,0:T(8,128)}, u32[]{:S(2)}) copy-start(f32[36,36,256]{1,2,0:T(8,128)} %copy.25) | copy-start | bytes 3981316
  43.6 12.2 %collective-permute-start.2 = (f32[36,36,1,18]{1,3,2,0:T(8,128)S(1)}, f32[36,36,1,18]{1,3,2,0:T(8,128)S(1)}, u32[]{:S(2)}, u32[]{:S(2)}) collective-permute-start(f32[36,36,1,18]{1,3,2,0:T(8,128)S(1)} %get-tuple-element.15), channel_id=1, source_target_pairs={{0,1},{1,2},{2,3},{3,4},{4,5},{5,6},{6,7},{7,8},{8,9},{9,10},{10,1... | collective-permute-start | bytes 279944 | tf_op jit(solution)/shard_map/ppermute | solution.py:14
  46.2 13.8 %collective-permute-start.3 = (f32[36,36,1,18]{1,3,2,0:T(8,128)S(1)}, f32[36,36,1,18]{1,3,2,0:T(8,128)S(1)}, u32[]{:S(2)}, u32[]{:S(2)}) collective-permute-start(f32[36,36,1,18]{1,3,2,0:T(8,128)S(1)} %get-tuple-element.16), channel_id=1, source_target_pairs={{1,0},{2,1},{3,2},{4,3},{5,4},{6,5},{7,6},{8,7},{9,8},{10,9},{11,1... | collective-permute-start | bytes 279944 | tf_op jit(solution)/shard_map/ppermute | solution.py:15
  65.7 8.0 %collective-permute-start.4 = (f32[36,36,16,1]{1,3,2,0:T(1,128)S(1)}, f32[36,36,16,1]{1,3,2,0:T(1,128)S(1)}, u32[]{:S(2)}, u32[]{:S(2)}) collective-permute-start(f32[36,36,16,1]{1,3,2,0:T(1,128)S(1)} %get-tuple-element.17), channel_id=1, source_target_pairs={{0,64},{64,128},{128,192},{192,256},{256,320},{320,384},{384,448},... | collective-permute-start | bytes 248840 | tf_op jit(solution)/shard_map/ppermute | solution.py:14
  67.6 7.9 %collective-permute-start.5 = (f32[36,36,16,1]{1,3,2,0:T(1,128)S(1)}, f32[36,36,16,1]{1,3,2,0:T(1,128)S(1)}, u32[]{:S(2)}, u32[]{:S(2)}) collective-permute-start(f32[36,36,16,1]{1,3,2,0:T(1,128)S(1)} %get-tuple-element.18), channel_id=1, source_target_pairs={{64,0},{128,64},{192,128},{256,192},{320,256},{384,320},{448,384},... | collective-permute-start | bytes 248840 | tf_op jit(solution)/shard_map/ppermute | solution.py:15
  75.6 13.4 %collective-permute-start.6 = (f32[36,36,1,18]{1,3,2,0:T(8,128)S(1)}, f32[36,36,1,18]{1,3,2,0:T(8,128)S(1)}, u32[]{:S(2)}, u32[]{:S(2)}) collective-permute-start(f32[36,36,1,18]{1,3,2,0:T(8,128)S(1)} %get-tuple-element.13), channel_id=1, source_target_pairs={{0,1},{1,2},{2,3},{3,4},{4,5},{5,6},{6,7},{7,8},{8,9},{9,10},{10,1... | collective-permute-start | bytes 279944 | tf_op jit(solution)/shard_map/ppermute | solution.py:14
  79.0 14.6 %collective-permute-start.7 = (f32[36,36,1,18]{1,3,2,0:T(8,128)S(1)}, f32[36,36,1,18]{1,3,2,0:T(8,128)S(1)}, u32[]{:S(2)}, u32[]{:S(2)}) collective-permute-start(f32[36,36,1,18]{1,3,2,0:T(8,128)S(1)} %get-tuple-element.14), channel_id=1, source_target_pairs={{1,0},{2,1},{3,2},{4,3},{5,4},{6,5},{7,6},{8,7},{9,8},{10,9},{11,1... | collective-permute-start | bytes 279944 | tf_op jit(solution)/shard_map/ppermute | solution.py:15
  106.7 19.7 %copy-start = (f32[36,36,16,16]{0,1,3,2:T(8,128)S(1)}, f32[36,36,16,16]{0,1,3,2:T(8,128)}, u32[]{:S(2)}) copy-start(f32[36,36,16,16]{0,1,3,2:T(8,128)} %copy.33) | copy-start | bytes 3981316
  150.2 35.7 %all-to-all-start.1 = ((f32[4,64,6]{2,0,1:T(4,128)}), f32[4,64,6]{2,0,1:T(4,128)S(1)}, u32[]{:S(2)}, u32[]{:S(2)}) async-start(f32[4,64,6]{2,0,1:T(4,128)} %copy.28), calls=%async_computation.1 | async-start | bytes 262144 | tf_op jit(solution)/shard_map/all_to_all | solution.py:76
where the time goes:
time: 188 us
  starting transfers between devices  55.2 us (29%)
  waiting for transfers between devices  48.9 us (26%)
  matrix products  40.4 us (21%)
  local copies, waits for them, and re-layouts  26.7 us (14%)
  other arithmetic  15.5 us (8%)
    dot_general x1, matrix products, body(): jnp.einsum('tkxy,t->kxy', energy, cosine, precision=lax.Precision.HIGHEST)  19.7 us
    ppermute x4, waiting for transfers between devices, with_halo(): before = lax.ppermute(last, axis, up)  18.6 us
    all_to_all x1, starting transfers between devices, body(): lax.all_to_all(outgoing, 'tile', split_axis=1, concat_axis=1, tiled=True)  18.6 us
    dot_general x1, matrix products, body(): jnp.einsum('tkxy,t->kxy', energy, sine, precision=lax.Precision.HIGHEST)  17.3 us
    all_to_all x1, starting transfers between devices, body(): lax.all_to_all(returning, 'tile', split_axis=1, concat_axis=1, tiled=True)  17 us
    all_to_all x1, waiting for transfers between devices, body(): lax.all_to_all(returning, 'tile', split_axis=1, concat_axis=1, tiled=True)  14.8 us
    mul x2, other arithmetic, body(): energy = factor[None] * advect(padded, east, north)  11.9 us
    ppermute x4, waiting for transfers between devices, with_halo(): after = lax.ppermute(initial, axis, down)  10.5 us
  transfers between devices with their start and end apart: 10, of which 8 were waited for; matrix products, arithmetic and copies ran while one was open for 7% of the time, Pallas kernels for 0%

commit v1 on v0

v1 whole, which is shorter than its diff:
```python
import functools
import math

import jax
import jax.numpy as jnp
from jax import lax
from jax.experimental import pallas as pl
from jax.experimental.pallas import tpu as pltpu
from jax.sharding import PartitionSpec as P

MESH = pl.DeviceIdType.MESH
F32 = jnp.float32
DIRS, FREQS, LANES, CELLS = 36, 36, 128, 256
SIDE = 16
NINE = 9
QUADS = ((0, 0), (1, 0), (1, 1), (0, 1))
X_START = (9, 0, 9, 0)


def dot(a, b, dims):
    return lax.dot_general(a, b, (dims, ((), ())), precision=lax.Precision.HIGHEST, preferred_element_type=F32)


def roll(value, shift):
    return pltpu.roll(value, shift, 1)


def kernel(
    n_grp, n_tile,
    spec_hbm, cour_hbm, decay_hbm, land_hbm, ice_hbm, route_hbm, source_hbm,
    out_hbm, coup_ref,
    e0, u0, cour_in, decay_in, land_in, ice_in, route_in, source_in,
    cos_tab, sin_tab, cour_ref, decay_ref, factor_ref, rate_ref, zonal_ref, merid_ref,
    xs, xr, xinfo_s, xinfo_r, ys, yr, cs, cr, yf_s, yf_r,
    rows_s, rows_r, back_s, back_r,
    in_sem, spec_sem, out_sem, send_sem, x_sem, xinfo_sem, y_sem, c_sem, yf_sem, rows_sem, back_sem,
):
    g = lax.axis_index("grp")
    t = lax.axis_index("tile")
    half = n_tile // 2

    def partner(n):
        step = (n + 1) // 2
        return lax.rem(t + half + jnp.where(n % 2 == 1, step, -step), n_tile)

    t_next, t_prev = lax.rem(t + 1, n_tile), lax.rem(t + n_tile - 1, n_tile)
    g_next, g_prev = lax.rem(g + 1, n_grp), lax.rem(g + n_grp - 1, n_grp)
    x_to = ((g, t_next), (g, t_prev))
    y_to = ((g_next, t), (g_prev, t))
    c_to = tuple((y_to[y][0], x_to[x][1]) for x, y in QUADS)

    barrier = pltpu.get_barrier_semaphore()

    def greet(n, carry):
        pl.semaphore_signal(barrier, inc=1, device_id=(g, partner(n)), device_id_type=MESH)
        return carry

    lax.fori_loop(0, n_tile - 1, greet, 0)
    for device in y_to + c_to:
        pl.semaphore_signal(barrier, inc=1, device_id=device, device_id_type=MESH)

    small = [
        pltpu.make_async_copy(src, dst, in_sem.at[i])
        for i, (src, dst) in enumerate((
            (ice_hbm, ice_in), (route_hbm, route_in), (cour_hbm, cour_in),
            (decay_hbm, decay_in), (land_hbm, land_in), (source_hbm, source_in),
        ))
    ]
    for copy in small:
        copy.start()
    big = [
        pltpu.make_async_copy(spec_hbm.at[pl.ds(NINE * q, NINE)], e0.at[pl.ds(NINE * q, NINE)], spec_sem.at[q])
        for q in range(4)
    ]
    for copy in big:
        copy.start()

    edge_x = (jnp.where(t > 0, 1.0, 0.0).astype(F32), jnp.where(t < n_tile - 1, 1.0, 0.0).astype(F32))
    edge_y = (jnp.where(g > 0, 1.0, 0.0).astype(F32), jnp.where(g < n_grp - 1, 1.0, 0.0).astype(F32))

    for j in range(DIRS):
        angle = 2.0 * math.pi * (j + 0.5) / DIRS
        cos_tab[j] = jnp.full((1, LANES), abs(math.cos(angle)), F32)
        sin_tab[j] = jnp.full((1, LANES), abs(math.sin(angle)), F32)
    for ref in (xs, ys, cs):
        ref[...] = jnp.zeros(ref.shape, F32)

    lane = lax.broadcasted_iota(jnp.int32, (FREQS, LANES), 1)
    slot16 = lane // SIDE
    pos16 = lane % SIDE
    freq = lax.broadcasted_iota(jnp.int32, (FREQS, LANES), 0).astype(F32)
    wavelen = jnp.exp(-0.2 * freq)

    for copy in small:
        copy.wait()

    eye = lax.broadcasted_iota(jnp.int32, (FREQS, FREQS), 0) == lax.broadcasted_iota(jnp.int32, (FREQS, FREQS), 1)

    def column(row):
        picked = jnp.where(eye, jnp.broadcast_to(row, (FREQS, FREQS)), 0.0)
        return jnp.broadcast_to(jnp.sum(picked, axis=1, keepdims=True), (FREQS, LANES))

    cour_ref[...] = column(cour_in[...])
    decay_ref[...] = column(decay_in[...])

    slot8 = lax.broadcasted_iota(jnp.int32, (8, CELLS), 0)
    tiles = lax.broadcasted_iota(jnp.int32, (n_tile, CELLS), 0)
    dest, dest_slot = route_in[0:1], route_in[1:2]
    to_dest = jnp.where(tiles == dest, 1.0, 0.0).astype(F32)
    lanes_of = jnp.concatenate(
        [jnp.where(slot8 == dest_slot, ice_in[c:c + 1], 0.0) for c in range(3)]
        + [jnp.zeros((LANES - 24, CELLS), F32)], axis=0)
    table = dot(to_dest, lanes_of, ((1,), (1,)))
    table = (
        pltpu.roll(table, 1, 0) + roll(table, 32) + roll(pltpu.roll(table, n_tile - 1, 0), 64)
    )
    rows_s[...] = table.reshape(n_tile, 1, LANES)

    cell_y = lax.broadcasted_iota(jnp.int32, (SIDE, CELLS), 1)
    row16 = lax.broadcasted_iota(jnp.int32, (SIDE, CELLS), 0)
    spread = jnp.where(cell_y % SIDE == row16, 1.0, 0.0).astype(F32)

    def flat(grid):
        wide = dot(grid.astype(F32), spread, ((1,), (0,)))
        return jnp.sum(jnp.where(cell_y // SIDE == row16, wide, 0.0), axis=0, keepdims=True)

    source, slot, land = flat(source_in[0]), flat(source_in[1]), flat(land_in[...])
    own = jnp.concatenate([source, slot, land, jnp.zeros((5, CELLS), F32)], axis=0)
    lane8 = lax.broadcasted_iota(jnp.int32, (8, LANES), 1)
    for side in range(2):
        if side == 0:
            edge = jnp.where(lane8 < SIDE, roll(own[:, LANES:], SIDE), 0.0)
        else:
            edge = jnp.where(lane8 < SIDE, own[:, :LANES], 0.0)
        for shift in (16, 32, 64):
            edge = edge + roll(edge, shift)
        xinfo_s[side] = edge

    def sides(q):
        return QUADS[q]

    def packed(q, j):
        i = X_START[q] + j
        group = i // 8
        return group, i - 8 * group

    def first(q):
        sx, sy = sides(q)

        def step(j, carry):
            d = NINE * q + j
            low, high = e0[d, :, 0:LANES], e0[d, :, LANES:CELLS]
            cour = cour_ref[...]
            ax, ay = cour * cos_tab[d], cour * sin_tab[d]
            keep = 1.0 - ax - ay
            if sx == 0:
                rl, rh = roll(low, SIDE), roll(high, SIDE)
                xl, xh = jnp.where(lane < SIDE, 0.0, rl), jnp.where(lane < SIDE, rl, rh)
            else:
                rl, rh = roll(low, LANES - SIDE), roll(high, LANES - SIDE)
                xl, xh = jnp.where(lane >= LANES - SIDE, rh, rl), jnp.where(lane >= LANES - SIDE, 0.0, rh)
            if sy == 0:
                yl = jnp.where(pos16 == 0, 0.0, roll(low, 1))
                yh = jnp.where(pos16 == 0, 0.0, roll(high, 1))
            else:
                yl = jnp.where(pos16 == SIDE - 1, 0.0, roll(low, LANES - 1))
                yh = jnp.where(pos16 == SIDE - 1, 0.0, roll(high, LANES - 1))
            ul = keep * low + ax * xl + ay * yl
            uh = keep * high + ax * xh + ay * yh
            u0[d, :, 0:LANES] = ul
            u0[d, :, LANES:CELLS] = uh
            group, place = packed(q, j)
            shift = lax.rem(16 * place + (16 if sx == 0 else 0), LANES)
            here = slot16 == place
            for kind, pair in enumerate(((low, high), (ul, uh))):
                edge = pair[1] if sx == 0 else pair[0]
                at = 3 * kind + group
                xs[sx, at] = jnp.where(here, roll(edge, shift), xs[sx, at])
            shift = lax.rem(j + (113 if sy == 0 else 0), LANES)
            here = pos16 == j
            arr = q % 2
            for kind, pair in enumerate(((low, high), (ul, uh))):
                at = 2 * kind + arr
                for part in range(2):
                    cut = slice(LANES * part, LANES * (part + 1))
                    ys[sy, at, :, cut] = jnp.where(here, roll(pair[part], shift), ys[sy, at, :, cut])
            corner = high if sx == 0 else low
            lies = (LANES - SIDE if sx == 0 else 0) + (SIDE - 1 if sy == 0 else 0)
            goes = 16 * place + (0 if sy == 0 else SIDE - 1)
            at = group - X_START[q] // 8
            cs[q, at] = jnp.where(lane == goes, roll(corner, lax.rem(goes - lies + LANES, LANES)), cs[q, at])
            goes = j + (0 if sx == 0 else LANES - SIDE)
            cs[q, 2] = jnp.where(lane == goes, roll(corner, lax.rem(goes - lies + LANES, LANES)), cs[q, 2])
            return carry

        lax.fori_loop(0, NINE, step, 0)

    for q in range(4):
        big[q].wait()
        first(q)

    pl.semaphore_wait(barrier, n_tile - 1 + 6)

    def send_row(src, dst, sem):
        def step(n, carry):
            d = partner(n)
            pltpu.make_async_remote_copy(
                src_ref=src.at[d], dst_ref=dst.at[t], send_sem=send_sem.at[0], recv_sem=sem.at[0],
                device_id=(g, d), device_id_type=MESH).start()
            return carry

        lax.fori_loop(0, n_tile - 1, step, 0)
        dst[pl.ds(t, 1)] = src[pl.ds(t, 1)]

    def rows_wait(ref, sem):
        view = ref.at[pl.ds(0, n_tile - 1)]
        pltpu.make_async_copy(view, view, sem.at[0]).wait()

    send_row(rows_s, rows_r, rows_sem)

    def remote(src, dst, sent, arrived, device):
        return pltpu.make_async_remote_copy(
            src_ref=src, dst_ref=dst, send_sem=sent, recv_sem=arrived, device_id=device, device_id_type=MESH)

    x_copy = [remote(xs.at[s], xr.at[s], send_sem.at[1 + s], x_sem.at[s], x_to[s]) for s in range(2)]
    i_copy = [remote(xinfo_s.at[s], xinfo_r.at[s], send_sem.at[3 + s], xinfo_sem.at[s], x_to[s]) for s in range(2)]
    y_copy = [remote(ys.at[s], yr.at[s], send_sem.at[5 + s], y_sem.at[s], y_to[s]) for s in range(2)]
    c_copy = [remote(cs.at[q], cr.at[q], send_sem.at[7 + q], c_sem.at[q], c_to[q]) for q in range(4)]
    for copy in i_copy + x_copy + y_copy + c_copy:
        copy.start()

    for copy in i_copy:
        copy.wait_recv()
    sources = jnp.concatenate([source, xinfo_r[0, 0:1], xinfo_r[1, 0:1]], axis=1)
    wide = lax.broadcasted_iota(jnp.int32, (n_tile, CELLS + 2 * LANES), 0).astype(F32)
    from_source = jnp.where(wide == sources, 1.0, 0.0).astype(F32)

    for copy in x_copy + y_copy + c_copy:
        copy.wait_recv()

    def halo_x(q, j, ref_value):
        sx, _ = sides(q)
        _, place = packed(q, j)
        shift = lax.rem((LANES if sx == 0 else 2 * LANES - SIDE) - 16 * place, LANES)
        return roll(ref_value, shift)

    def halo_y(q, j, value):
        _, sy = sides(q)
        return roll(value, lax.rem((LANES if sy == 0 else LANES + SIDE - 1) - j, LANES))

    def second(q):
        sx, sy = sides(q)

        def step(j, carry):
            d = NINE * q + j
            cour = cour_ref[...]
            ax, ay = cour * cos_tab[d] * edge_x[sx], cour * sin_tab[d] * edge_y[sy]
            group, _ = packed(q, j)
            hx = ax * halo_x(q, j, xr[sx, group])
            rim = pos16 == (0 if sy == 0 else SIDE - 1)
            hl = jnp.where(rim, ay * halo_y(q, j, yr[sy, q % 2, :, 0:LANES]), 0.0)
            hh = jnp.where(rim, ay * halo_y(q, j, yr[sy, q % 2, :, LANES:CELLS]), 0.0)
            if sx == 0:
                hl = hl + jnp.where(lane < SIDE, hx, 0.0)
            else:
                hh = hh + jnp.where(lane >= LANES - SIDE, hx, 0.0)
            u0[d, :, 0:LANES] = u0[d, :, 0:LANES] + hl
            u0[d, :, LANES:CELLS] = u0[d, :, LANES:CELLS] + hh
            return carry

        lax.fori_loop(0, NINE, step, 0)

    for q in range(4):
        second(q)

    turn = [10.0 * (j + 0.5) * math.pi / 180.0 for j in range(NINE)]
    for group in range(3):
        weight = jnp.zeros((FREQS, LANES), F32)
        for place in range(8):
            i = 8 * group + place
            if i < 18:
                value = math.cos(turn[i]) if i < NINE else math.sin(turn[i - NINE])
                weight = jnp.where(slot16 == place, value, weight)
        weight = weight * cour_ref[...]
        for q in range(4):
            sx, sy = sides(q)
            at = group - X_START[q] // 8
            if 0 <= at < 2:
                xr[sx, 3 + group] = xr[sx, 3 + group] + weight * (edge_y[sy] * cr[q, at])
    for arr in range(2):
        weight = jnp.zeros((FREQS, LANES), F32)
        for j in range(NINE):
            weight = jnp.where(pos16 == j, math.cos(turn[j]) if arr == 0 else math.sin(turn[j]), weight)
        weight = weight * cour_ref[...]
        for q in (arr, arr + 2):
            sx, sy = sides(q)
            cut = slice(0, LANES) if sx == 0 else slice(LANES, CELLS)
            yr[sy, 2 + arr, :, cut] = yr[sy, 2 + arr, :, cut] + weight * (edge_x[sx] * cr[q, 2])

    rows_wait(rows_r, rows_sem)
    arrived = rows_r[...].reshape(n_tile, LANES).T
    found = dot(arrived, from_source, ((1,), (0,)))

    def pick(section, cut, slots):
        width = slots.shape[1]
        mask = lax.broadcasted_iota(jnp.int32, (8, width), 0).astype(F32) == slots
        return [
            jnp.sum(jnp.where(mask, found[32 * section + 8 * c:32 * section + 8 * c + 8, cut], 0.0), axis=0, keepdims=True)
            for c in range(3)
        ]

    field = pick(1, slice(0, CELLS), slot)
    near = [
        pick(2 * s, slice(CELLS + LANES * s, CELLS + LANES * (s + 1)), xinfo_r[s, 1:2]) for s in range(2)
    ]

    fields = jnp.concatenate(field + [land, jnp.zeros((4, CELLS), F32)], axis=0)
    pos8 = lane8 % SIDE
    for s in range(2):
        for part in range(2):
            cut = slice(LANES * part, LANES * (part + 1))
            edge = jnp.where(pos8 == (SIDE - 1 if s == 0 else 0), fields[:, cut], 0.0)
            for shift in (1, 2, 4, 8):
                edge = edge + roll(edge, LANES - shift if s == 0 else shift)
            yf_s[s, :, cut] = edge
    f_copy = [remote(yf_s.at[s], yf_r.at[s], send_sem.at[11 + s], yf_sem.at[s], y_to[s]) for s in range(2)]
    for copy in f_copy:
        copy.start()

    def rate_of(values):
        conc, thick, floe = values
        return decay_ref[...] * conc * (thick + wavelen / (wavelen + floe))

    for part in range(2):
        cut = slice(LANES * part, LANES * (part + 1))
        rate = rate_of([v[:, cut] for v in field])
        rate_ref[:, cut] = rate
        factor_ref[:, cut] = land[:, cut] * jnp.exp(-rate)
    for s in range(2):
        rim = (xinfo_r[s, 2:3] * edge_x[s]) * jnp.exp(-rate_of(near[s]))
        for group in range(3):
            xr[s, 3 + group] = xr[s, 3 + group] * rim

    def scale(d, carry):
        u0[d] = u0[d] * factor_ref[...]
        return carry

    lax.fori_loop(0, DIRS, scale, 0)

    for copy in f_copy:
        copy.wait_recv()
    for s in range(2):
        for part in range(2):
            cut = slice(LANES * part, LANES * (part + 1))
            rim = (yf_r[s, 3:4, cut] * edge_y[s]) * jnp.exp(-rate_of([yf_r[s, c:c + 1, cut] for c in range(3)]))
            for arr in range(2):
                yr[s, 2 + arr, :, cut] = yr[s, 2 + arr, :, cut] * rim

    zonal_ref[...] = jnp.zeros((FREQS, CELLS), F32)
    merid_ref[...] = jnp.zeros((FREQS, CELLS), F32)

    def third(q):
        sx, sy = sides(q)

        def step(j, carry):
            d = NINE * q + j
            low, high = u0[d, :, 0:LANES], u0[d, :, LANES:CELLS]
            cour = cour_ref[...]
            cx, sn = cos_tab[d], sin_tab[d]
            ax, ay = cour * cx, cour * sn
            keep = 1.0 - ax - ay
            group, _ = packed(q, j)
            hx = halo_x(q, j, xr[sx, 3 + group])
            if sx == 0:
                rl, rh = roll(low, SIDE), roll(high, SIDE)
                xl, xh = jnp.where(lane < SIDE, hx, rl), jnp.where(lane < SIDE, rl, rh)
            else:
                rl, rh = roll(low, LANES - SIDE), roll(high, LANES - SIDE)
                xl, xh = jnp.where(lane >= LANES - SIDE, rh, rl), jnp.where(lane >= LANES - SIDE, hx, rh)
            shift, rim = (1, pos16 == 0) if sy == 0 else (LANES - 1, pos16 == SIDE - 1)
            hl = halo_y(q, j, yr[sy, 2 + q % 2, :, 0:LANES])
            hh = halo_y(q, j, yr[sy, 2 + q % 2, :, LANES:CELLS])
            yl = jnp.where(rim, hl, roll(low, shift))
            yh = jnp.where(rim, hh, roll(high, shift))
            nl = factor_ref[:, 0:LANES] * (keep * low + ax * xl + ay * yl)
            nh = factor_ref[:, LANES:CELLS] * (keep * high + ax * xh + ay * yh)
            e0[d, :, 0:LANES] = nl
            e0[d, :, LANES:CELLS] = nh
            sc = cx if sx == 0 else -cx
            ss = sn if sy == 0 else -sn
            zonal_ref[:, 0:LANES] += sc * nl
            zonal_ref[:, LANES:CELLS] += sc * nh
            merid_ref[:, 0:LANES] += ss * nl
            merid_ref[:, LANES:CELLS] += ss * nh
            return carry

        lax.fori_loop(0, NINE, step, 0)

    result = [
        pltpu.make_async_copy(e0.at[pl.ds(NINE * q, NINE)], out_hbm.at[pl.ds(NINE * q, NINE)], out_sem.at[q])
        for q in range(4)
    ]
    for q in range(4):
        third(q)
        result[q].start()

    raw = jnp.exp(0.1 * freq)
    weight = 3.0 * raw / jnp.sum(raw, axis=0, keepdims=True)
    values = []
    for scaled in (False, True):
        for ref in (zonal_ref, merid_ref):
            parts = []
            for part in range(2):
                cut = slice(LANES * part, LANES * (part + 1))
                total = jnp.sum((rate_ref[:, cut] if scaled else weight) * ref[:, cut], axis=0, keepdims=True)
                parts.append(total * (4.0 / FREQS) if scaled else total)
            values.append(jnp.concatenate(parts, axis=1))
    picked = slot8.astype(F32) == slot
    lanes_of = jnp.concatenate(
        [jnp.where(picked, v, 0.0) for v in values] + [jnp.zeros((LANES - 32, CELLS), F32)], axis=0)
    back_s[...] = dot(from_source[:, 0:CELLS], lanes_of, ((1,), (1,))).reshape(n_tile, 1, LANES)
    rows_wait(rows_s, send_sem)
    send_row(back_s, back_r, back_sem)

    rows_wait(back_r, back_sem)
    found = dot(back_r[...].reshape(n_tile, LANES).T, to_dest, ((1,), (0,)))
    for c in range(4):
        coup_ref[c:c + 1] = jnp.sum(
            jnp.where(slot8 == dest_slot, found[8 * c:8 * c + 8], 0.0), axis=0, keepdims=True)

    rows_wait(back_s, send_sem)
    for copy in x_copy + i_copy + y_copy + c_copy + f_copy:
        copy.wait_send()
    for copy in result:
        copy.wait()


def solution(mesh):
    n_grp, n_tile = mesh.shape["grp"], mesh.shape["tile"]

    def body(spectrum, courant, decay, land, ice_rows, ice_route, wave_source):
        vmem = pltpu.VMEM
        dma = pltpu.SemaphoreType.DMA
        scratch = [
            vmem((DIRS, FREQS, CELLS), F32), vmem((DIRS, FREQS, CELLS), F32),
            vmem((1, FREQS), F32), vmem((1, FREQS), F32), vmem((SIDE, SIDE), jnp.int32),
            vmem((3, CELLS), F32), vmem((2, CELLS), jnp.int32), vmem((2, SIDE, SIDE), jnp.int32),
            vmem((DIRS, 1, LANES), F32), vmem((DIRS, 1, LANES), F32),
            vmem((FREQS, LANES), F32), vmem((FREQS, LANES), F32),
            vmem((FREQS, CELLS), F32), vmem((FREQS, CELLS), F32),
            vmem((FREQS, CELLS), F32), vmem((FREQS, CELLS), F32),
            vmem((2, 6, FREQS, LANES), F32), vmem((2, 6, FREQS, LANES), F32),
            vmem((2, 8, LANES), F32), vmem((2, 8, LANES), F32),
            vmem((2, 4, FREQS, CELLS), F32), vmem((2, 4, FREQS, CELLS), F32),
            vmem((4, 3, FREQS, LANES), F32), vmem((4, 3, FREQS, LANES), F32),
            vmem((2, 8, CELLS), F32), vmem((2, 8, CELLS), F32),
            vmem((n_tile, 1, LANES), F32), vmem((n_tile, 1, LANES), F32),
            vmem((n_tile, 1, LANES), F32), vmem((n_tile, 1, LANES), F32),
            dma((6,)), dma((4,)), dma((4,)), dma((13,)), dma((2,)), dma((2,)), dma((2,)), dma((4,)), dma((2,)),
            dma((1,)), dma((1,)),
        ]
        return pl.pallas_call(
            functools.partial(kernel, n_grp, n_tile),
            out_shape=(
                jax.ShapeDtypeStruct((DIRS, FREQS, CELLS), F32),
                jax.ShapeDtypeStruct((4, CELLS), F32),
            ),
            in_specs=[pl.BlockSpec(memory_space=pl.ANY)] * 7,
            out_specs=(pl.BlockSpec(memory_space=pl.ANY), pl.BlockSpec(memory_space=pltpu.VMEM)),
            scratch_shapes=scratch,
            name="coupling_step",
            compiler_params=pltpu.CompilerParams(
                collective_id=0, has_side_effects=True, vmem_limit_bytes=60 * 1024 * 1024),
        )(spectrum, courant.reshape(1, FREQS), decay.reshape(1, FREQS), land, ice_rows, ice_route, wave_source)

    in_specs = (
        P(None, None, ("grp", "tile")),
        P(),
        P(),
        P("tile", "grp"),
        P(None, ("grp", "tile")),
        P(None, ("grp", "tile")),
        P(None, "tile", "grp"),
    )
    out_specs = (P(None, None, ("grp", "tile")), P(None, ("grp", "tile")))
    return jax.shard_map(body, mesh=mesh, in_specs=in_specs, out_specs=out_specs, check_vma=False)
```

time: 188 us -> 53.7 us (0.29)
  the two profiles are of different devices: /device:TPU:8 before, /device:TPU:1 now
where the time goes in v1:
time: 53.7 us; the launch traced here: 53.5 us
  Pallas kernels  49.7 us (93%)
  local copies, waits for them, and re-layouts  3.18 us (6%)
  between operations  0.65 us (1%)
    pallas_call x1, Pallas kernels, body(): pl.pallas_call(functools.partial(kernel, n_grp, n_tile), out_shape=(jax.S...  49.7 us
    unnamed x4, local copies, waits for them, and re-layouts  3.18 us

profile of v1, /device:TPU:1, one launch (start us, length us, event | category | flops | bytes accessed | tf_op | source)
XLA Modules:
  0.0 53.5 jit_solution(10071586784539673512)
XLA Ops:
  0.6 49.7 %coupling_step.1 = (f32[36,36,256]{2,1,0:T(8,128)}, f32[4,256]{1,0:T(4,128)}) custom-call(f32[36,36,256]{2,1,0:T(8,128)} %spec_hbm.1, f32[1,36]{1,0:T(1,128)} %bitcast.2, f32[1,36]{1,0:T(1,128)} %bitcast.3, s32[16,16]{1,0:T(8,128)} %land_hbm.1, f32[3,256]{1,0:T(4,128)} %ice_hbm.1, s32[2,256]{1,0:T(2,128)} %route_hbm.1, s32[2,16,16]{2,1,0:T(8,128)} %source_hbm.1), custom_call_target="tpu_custom_call" | custom-call | tf_op jit(solution)/shard_map/coupling_step/pallas_call | solution.py:462
  50.3 0.0 copy-start
  50.3 2.6 %copy.11 = f32[36,36,256]{2,1,0:T(8,128)} copy(f32[36,36,256]{2,1,0:T(8,128)} %get-tuple-element.4) | data formatting | bytes 2654208
  52.9 0.0 copy-done
  52.9 0.6 %copy.12 = f32[4,256]{1,0:T(4,128)} copy(f32[4,256]{1,0:T(4,128)S(1)} %copy-done) | data formatting | bytes 8192
Async XLA Ops:
  50.3 2.6 %copy-start = (f32[4,256]{1,0:T(4,128)S(1)}, f32[4,256]{1,0:T(4,128)}, u32[]{:S(2)}) copy-start(f32[4,256]{1,0:T(4,128)} %get-tuple-element.5) | copy-start | bytes 12292

commit v2 on v1

v2 whole, which is shorter than its diff:
```python
import functools
import math

import jax
import jax.numpy as jnp
from jax import lax
from jax.experimental import pallas as pl
from jax.experimental.pallas import tpu as pltpu
from jax.sharding import PartitionSpec as P

MESH = pl.DeviceIdType.MESH
F32 = jnp.float32
DIRS, FREQS, LANES, CELLS = 36, 36, 128, 256
SIDE = 16
NINE = 9
QUADS = ((0, 0), (1, 0), (1, 1), (0, 1))
X_START = (9, 0, 9, 0)
TURN = [(j + 0.5) * math.pi / 18.0 for j in range(NINE)]
HALVES = (slice(0, LANES), slice(LANES, CELLS))


def size(q, j):
    pair = math.cos(TURN[j]), math.sin(TURN[j])
    return pair if q % 2 == 0 else pair[::-1]


def place_of(q, j):
    return divmod(X_START[q] + j, 8)


def dot(a, b, dims):
    return lax.dot_general(a, b, (dims, ((), ())), precision=lax.Precision.HIGHEST, preferred_element_type=F32)


def roll(value, shift):
    shift %= value.shape[1]
    return pltpu.roll(value, shift, 1) if shift else value


def kernel(
    n_grp, n_tile,
    spec_hbm, cour_hbm, decay_hbm, land_hbm, ice_hbm, route_hbm, source_hbm,
    e0, back_r,
    u0, cour_in, decay_in, land_in, ice_in, route_in, source_in,
    weights, cour_ref, decay_ref, factor_ref, rate_ref, zonal_ref, merid_ref,
    xs, xr, xinfo_s, xinfo_r, ys, yr, cs, cr, yf_s, yf_r,
    rows_s, rows_r, back_s,
    in_sem, spec_sem, send_sem, x_sem, xinfo_sem, y_sem, c_sem, yf_sem, rows_sem, back_sem,
):
    g = lax.axis_index("grp")
    t = lax.axis_index("tile")
    half = n_tile // 2

    def partner(n):
        step = (n + 1) // 2
        return lax.rem(t + half + jnp.where(n % 2 == 1, step, -step), n_tile)

    t_next, t_prev = lax.rem(t + 1, n_tile), lax.rem(t + n_tile - 1, n_tile)
    g_next, g_prev = lax.rem(g + 1, n_grp), lax.rem(g + n_grp - 1, n_grp)
    x_to = ((g, t_next), (g, t_prev))
    y_to = ((g_next, t), (g_prev, t))
    c_to = tuple((y_to[y][0], x_to[x][1]) for x, y in QUADS)

    barrier = pltpu.get_barrier_semaphore()

    def greet(n, carry):
        pl.semaphore_signal(barrier, inc=1, device_id=(g, partner(n)), device_id_type=MESH)
        return carry

    lax.fori_loop(0, n_tile - 1, greet, 0)
    for device in y_to + c_to:
        pl.semaphore_signal(barrier, inc=1, device_id=device, device_id_type=MESH)

    small = [
        pltpu.make_async_copy(src, dst, in_sem.at[i])
        for i, (src, dst) in enumerate((
            (ice_hbm, ice_in), (route_hbm, route_in), (cour_hbm, cour_in),
            (decay_hbm, decay_in), (land_hbm, land_in), (source_hbm, source_in),
        ))
    ]
    for copy in small:
        copy.start()
    big = [
        pltpu.make_async_copy(spec_hbm.at[pl.ds(NINE * q, NINE)], e0.at[pl.ds(NINE * q, NINE)], spec_sem.at[q])
        for q in range(4)
    ]
    for copy in big:
        copy.start()

    edge_x = (jnp.where(t > 0, 1.0, 0.0).astype(F32), jnp.where(t < n_tile - 1, 1.0, 0.0).astype(F32))
    edge_y = (jnp.where(g > 0, 1.0, 0.0).astype(F32), jnp.where(g < n_grp - 1, 1.0, 0.0).astype(F32))

    def masks(height):
        lane = lax.broadcasted_iota(jnp.int32, (height, LANES), 1)
        slot16, pos16 = lane // SIDE, lane % SIDE
        return lane, slot16, pos16, (lane < SIDE, lane >= LANES - SIDE), (pos16 == 0, pos16 == SIDE - 1)

    lane, slot16, pos16, _, _ = masks(8)

    for group in range(3):
        for kind in range(2):
            weight = jnp.zeros((8, LANES), F32)
            for q in (0, 1):
                for j in range(NINE):
                    if place_of(q, j)[0] == group:
                        weight = jnp.where(slot16 == place_of(q, j)[1], size(q, j)[kind], weight)
            weights[3 * kind + group] = weight
    for arr in range(2):
        for kind in range(2):
            weight = jnp.zeros((8, LANES), F32)
            for j in range(NINE):
                weight = jnp.where(pos16 == j, size(arr, j)[kind], weight)
            weights[6 + 2 * kind + arr] = weight

    for copy in small:
        copy.wait()

    eye = lax.broadcasted_iota(jnp.int32, (FREQS, FREQS), 0) == lax.broadcasted_iota(jnp.int32, (FREQS, FREQS), 1)

    def column(row):
        picked = jnp.where(eye, jnp.broadcast_to(row, (FREQS, FREQS)), 0.0)
        return jnp.broadcast_to(jnp.sum(picked, axis=1, keepdims=True), (FREQS, LANES))

    cour_ref[...] = column(cour_in[...])
    decay_ref[...] = column(decay_in[...])

    slot8 = lax.broadcasted_iota(jnp.int32, (8, CELLS), 0)
    tiles = lax.broadcasted_iota(jnp.int32, (n_tile, CELLS), 0)
    dest, dest_slot = route_in[0:1], route_in[1:2]
    to_dest = jnp.where(tiles == dest, 1.0, 0.0).astype(F32)
    lanes_of = jnp.concatenate(
        [jnp.where(slot8 == dest_slot, ice_in[c:c + 1], 0.0) for c in range(3)]
        + [jnp.zeros((LANES - 24, CELLS), F32)], axis=0)
    table = dot(to_dest, lanes_of, ((1,), (1,)))
    table = (
        pltpu.roll(table, 1, 0) + roll(table, 32) + roll(pltpu.roll(table, n_tile - 1, 0), 64)
    )
    rows_s[...] = table.reshape(n_tile, 1, LANES)

    cell_y = lax.broadcasted_iota(jnp.int32, (SIDE, CELLS), 1)
    row16 = lax.broadcasted_iota(jnp.int32, (SIDE, CELLS), 0)
    spread = jnp.where(cell_y % SIDE == row16, 1.0, 0.0).astype(F32)

    def flat(grid):
        wide = dot(grid.astype(F32), spread, ((1,), (0,)))
        return jnp.sum(jnp.where(cell_y // SIDE == row16, wide, 0.0), axis=0, keepdims=True)

    source, slot, land = flat(source_in[0]), flat(source_in[1]), flat(land_in[...])
    own = jnp.concatenate([source, slot, land, jnp.zeros((5, CELLS), F32)], axis=0)
    for side in range(2):
        if side == 0:
            edge = jnp.where(lane < SIDE, roll(own[:, LANES:], SIDE), 0.0)
        else:
            edge = jnp.where(lane < SIDE, own[:, :LANES], 0.0)
        for shift in (16, 32, 64):
            edge = edge + roll(edge, shift)
        xinfo_s[side] = edge

    def each_tile(body, carry=()):
        def step(n, carry):
            return tuple(a + b for a, b in zip(carry, body(pl.ds(pl.multiple_of(8 * n, 8), 8))))

        whole = FREQS // 8
        carry = lax.fori_loop(0, whole, step, carry)
        rest = body(pl.ds(8 * whole, FREQS - 8 * whole))
        return [jnp.sum(a, axis=0, keepdims=True) + jnp.sum(b, axis=0, keepdims=True) for a, b in zip(carry, rest)]

    def moved_x(first_x, sx, low, high, edge_low, edge_high):
        if sx == 0:
            rl, rh = roll(low, SIDE), roll(high, SIDE)
            return jnp.where(first_x[0], edge_low, rl), jnp.where(first_x[0], rl, rh)
        rl, rh = roll(low, -SIDE), roll(high, -SIDE)
        return jnp.where(first_x[1], rh, rl), jnp.where(first_x[1], edge_high, rh)

    def moved_y(first_y, sy, value):
        return jnp.where(first_y[sy], 0.0, roll(value, 1 if sy == 0 else -1))

    def halo_x(q, j, message):
        return roll(message, (0 if q in (0, 3) else LANES - SIDE) - SIDE * place_of(q, j)[1])

    def halo_y(q, j, message):
        return roll(message, (0 if q < 2 else SIDE - 1) - j)

    for copy in big:
        copy.wait()

    def first():
        _, slot16, pos16, first_x, first_y = masks(FREQS)
        cour = cour_ref[...]
        for q in (3, 0, 1, 2):
            sx, sy = QUADS[q]
            for j in range(NINE):
                d = NINE * q + j
                low, high = e0[d, :, HALVES[0]], e0[d, :, HALVES[1]]
                cx, sn = size(q, j)
                ax, ay = cour * cx, cour * sn
                keep = 1.0 - cour * (cx + sn)
                xl, xh = moved_x(first_x, sx, low, high, 0.0, 0.0)
                ul = keep * low + ax * xl + ay * moved_y(first_y, sy, low)
                uh = keep * high + ax * xh + ay * moved_y(first_y, sy, high)
                u0[d, :, HALVES[0]] = ul
                u0[d, :, HALVES[1]] = uh
                group, place = place_of(q, j)
                for kind, pair in enumerate(((low, high), (ul, uh))):
                    edge = roll(pair[1], SIDE * place + SIDE) if sx == 0 else roll(pair[0], SIDE * place)
                    at = 3 * kind + group
                    xs[sx, at] = jnp.where(slot16 == place, edge, xs[sx, at] if place else 0.0)
                    at = 2 * kind + q % 2
                    for half in range(2):
                        cut = HALVES[half]
                        edge = roll(pair[half], j - (SIDE - 1 if sy == 0 else 0))
                        ys[sy, at, :, cut] = jnp.where(pos16 == j, edge, ys[sy, at, :, cut] if j else 0.0)
        for q in range(4):
            sx, sy = QUADS[q]
            cs[q, 2] = roll(ys[sy, q % 2, :, HALVES[1 - sx]], SIDE if sx == 0 else -SIDE)
            for n in range(2):
                group = X_START[q] // 8 + n
                lies = [place_of(q, j)[1] for j in range(NINE) if place_of(q, j)[0] == group]
                mine = (slot16 >= lies[0]) & (slot16 <= lies[-1]) & first_y[sy]
                cs[q, n] = jnp.where(mine, roll(xs[sx, group], 1 - SIDE if sy == 0 else SIDE - 1), 0.0)

    first()

    pl.semaphore_wait(barrier, n_tile - 1 + 6)

    def send_row(src, dst, sem):
        def step(n, carry):
            d = partner(n)
            pltpu.make_async_remote_copy(
                src_ref=src.at[d], dst_ref=dst.at[t], send_sem=send_sem.at[0], recv_sem=sem.at[0],
                device_id=(g, d), device_id_type=MESH).start()
            return carry

        lax.fori_loop(0, n_tile - 1, step, 0)
        dst[pl.ds(t, 1)] = src[pl.ds(t, 1)]

    def rows_wait(ref, sem):
        view = ref.at[pl.ds(0, n_tile - 1)]
        pltpu.make_async_copy(view, view, sem.at[0]).wait()

    send_row(rows_s, rows_r, rows_sem)

    def remote(src, dst, sent, arrived, device):
        return pltpu.make_async_remote_copy(
            src_ref=src, dst_ref=dst, send_sem=sent, recv_sem=arrived, device_id=device, device_id_type=MESH)

    x_copy = [remote(xs.at[s], xr.at[s], send_sem.at[1 + s], x_sem.at[s], x_to[s]) for s in range(2)]
    i_copy = [remote(xinfo_s.at[s], xinfo_r.at[s], send_sem.at[3 + s], xinfo_sem.at[s], x_to[s]) for s in range(2)]
    y_copy = [remote(ys.at[s], yr.at[s], send_sem.at[5 + s], y_sem.at[s], y_to[s]) for s in range(2)]
    c_copy = [remote(cs.at[q], cr.at[q], send_sem.at[7 + q], c_sem.at[q], c_to[q]) for q in range(4)]
    for copy in i_copy + x_copy + y_copy + c_copy:
        copy.start()

    for copy in i_copy:
        copy.wait_recv()
    sources = jnp.concatenate([source, xinfo_r[0, 0:1], xinfo_r[1, 0:1]], axis=1)
    wide = lax.broadcasted_iota(jnp.int32, (n_tile, CELLS + 2 * LANES), 0).astype(F32)
    from_source = jnp.where(wide == sources, 1.0, 0.0).astype(F32)

    for copy in x_copy + y_copy + c_copy:
        copy.wait_recv()

    def second(rows):
        _, slot16, pos16, first_x, first_y = masks(rows.size)
        cour = cour_ref[rows]
        x_weight = [cour * weights[i, 0:rows.size] for i in range(6)]
        y_weight = [cour * weights[6 + i, 0:rows.size] for i in range(4)]
        for q in range(4):
            sx, sy = QUADS[q]
            x_edge = [x_weight[n] * (xr[sx, n, rows] * edge_x[sx]) for n in range(3)]
            y_edge = [y_weight[2 + q % 2] * (yr[sy, q % 2, rows, cut] * edge_y[sy]) for cut in HALVES]
            for j in range(NINE):
                d = NINE * q + j
                add = [jnp.where(first_y[sy], halo_y(q, j, y_edge[half]), 0.0) for half in range(2)]
                add[sx] = add[sx] + jnp.where(first_x[sx], halo_x(q, j, x_edge[place_of(q, j)[0]]), 0.0)
                for half in range(2):
                    u0[d, rows, HALVES[half]] = u0[d, rows, HALVES[half]] + add[half]
        for sx in range(2):
            corner = [jnp.zeros((rows.size, LANES), F32)] * 3
            for q in range(4):
                if QUADS[q][0] == sx:
                    for n in range(2):
                        group = X_START[q] // 8 + n
                        corner[group] = corner[group] + edge_y[QUADS[q][1]] * cr[q, n, rows]
            for n in range(3):
                whole = xr[sx, 3 + n, rows] + x_weight[3 + n] * corner[n]
                xr[sx, 3 + n, rows] = whole * (x_weight[n] * edge_x[sx])
        for q in range(4):
            sx, sy = QUADS[q]
            for half in range(2):
                whole = yr[sy, 2 + q % 2, rows, HALVES[half]]
                if half == sx:
                    corner = jnp.where(slot16 == (0 if sx == 0 else 7), cr[q, 2, rows], 0.0)
                    whole = whole + y_weight[q % 2] * (edge_x[sx] * corner)
                yr[sy, 2 + q % 2, rows, HALVES[half]] = whole * (y_weight[2 + q % 2] * edge_y[sy])
        return ()

    each_tile(second)

    rows_wait(rows_r, rows_sem)
    arrived = rows_r[...].reshape(n_tile, LANES).T
    found = dot(arrived, from_source, ((1,), (0,)))

    def pick(section, cut, slots):
        width = slots.shape[1]
        mask = lax.broadcasted_iota(jnp.int32, (8, width), 0).astype(F32) == slots
        return [
            jnp.sum(jnp.where(mask, found[32 * section + 8 * c:32 * section + 8 * c + 8, cut], 0.0), axis=0, keepdims=True)
            for c in range(3)
        ]

    field = pick(1, slice(0, CELLS), slot)
    near = [
        pick(2 * s, slice(CELLS + LANES * s, CELLS + LANES * (s + 1)), xinfo_r[s, 1:2]) for s in range(2)
    ]

    fields = jnp.concatenate(field + [land, jnp.zeros((4, CELLS), F32)], axis=0)
    for s in range(2):
        for part in range(2):
            cut = slice(LANES * part, LANES * (part + 1))
            edge = jnp.where(pos16 == (SIDE - 1 if s == 0 else 0), fields[:, cut], 0.0)
            for shift in (1, 2, 4, 8):
                edge = edge + roll(edge, -shift if s == 0 else shift)
            yf_s[s, :, cut] = edge
    f_copy = [remote(yf_s.at[s], yf_r.at[s], send_sem.at[11 + s], yf_sem.at[s], y_to[s]) for s in range(2)]
    for copy in f_copy:
        copy.start()

    def rate_of(rows, values):
        conc, thick, floe = values
        wavelen = jnp.exp(-0.2 * (lax.broadcasted_iota(jnp.int32, (rows.size, LANES), 0) + rows.start).astype(F32))
        return decay_ref[rows] * conc * (thick + wavelen / (wavelen + floe))

    near_land = [xinfo_r[s, 2:3] for s in range(2)]

    def third(rows):
        _, slot16, pos16, first_x, first_y = masks(rows.size)
        cour = cour_ref[rows]
        factor = []
        for half in range(2):
            cut = HALVES[half]
            rate = rate_of(rows, [v[:, cut] for v in field])
            rate_ref[rows, cut] = rate
            factor.append(land[:, cut] * jnp.exp(-rate))
            factor_ref[rows, cut] = factor[half]
        zonal, merid = [0.0, 0.0], [0.0, 0.0]
        for sx in range(2):
            rim = near_land[sx] * jnp.exp(-rate_of(rows, near[sx]))
            message = [xr[sx, 3 + n, rows] * rim for n in range(3)]
            for q in range(4):
                if QUADS[q][0] != sx:
                    continue
                sy = QUADS[q][1]
                for j in range(NINE):
                    d = NINE * q + j
                    low, high = u0[d, rows, HALVES[0]] * factor[0], u0[d, rows, HALVES[1]] * factor[1]
                    cx, sn = size(q, j)
                    ax, ay = cour * cx, cour * sn
                    keep = 1.0 - cour * (cx + sn)
                    hx = halo_x(q, j, message[place_of(q, j)[0]])
                    xl, xh = moved_x(first_x, sx, ax * low, ax * high, hx, hx)
                    new = (
                        factor[0] * (keep * low + xl + ay * moved_y(first_y, sy, low)),
                        factor[1] * (keep * high + xh + ay * moved_y(first_y, sy, high)),
                    )
                    for half in range(2):
                        e0[d, rows, HALVES[half]] = new[half]
                        zonal[half] = zonal[half] + (cx if sx == 0 else -cx) * new[half]
                        merid[half] = merid[half] + (sn if sy == 0 else -sn) * new[half]
        for half in range(2):
            zonal_ref[rows, HALVES[half]] = zonal[half]
            merid_ref[rows, HALVES[half]] = merid[half]
        return ()

    each_tile(third)

    for copy in f_copy:
        copy.wait_recv()

    raw_sum = sum(math.exp(0.1 * k) for k in range(FREQS))

    def fourth(rows):
        _, _, pos16, _, first_y = masks(rows.size)
        weight_of = [weights[6 + i, 0:rows.size] for i in range(4)]
        factor = [factor_ref[rows, cut] for cut in HALVES]
        zonal = [zonal_ref[rows, cut] for cut in HALVES]
        merid = [merid_ref[rows, cut] for cut in HALVES]
        for sy in range(2):
            inner = [jnp.where(first_y[sy], f, 0.0) for f in factor]
            message = [[], []]
            for half in range(2):
                cut = HALVES[half]
                rim = yf_r[sy, 3:4, cut] * jnp.exp(-rate_of(rows, [yf_r[sy, c:c + 1, cut] for c in range(3)]))
                message[half] = [yr[sy, 2 + arr, rows, cut] * rim for arr in range(2)]
            for q in (2 * sy, 2 * sy + 1):
                for j in range(NINE):
                    d = NINE * q + j
                    for half in range(2):
                        cut = HALVES[half]
                        e0[d, rows, cut] = e0[d, rows, cut] + inner[half] * halo_y(q, j, message[half][q % 2])
            for half in range(2):
                pair = message[half]
                sign = [1.0 if QUADS[2 * sy + arr][0] == 0 else -1.0 for arr in range(2)]
                along = sign[0] * weight_of[0] * pair[0] + sign[1] * weight_of[1] * pair[1]
                across = weight_of[2] * pair[0] + weight_of[3] * pair[1]
                if sy == 1:
                    across = -across
                for total, part in ((zonal, along), (merid, across)):
                    part = jnp.where(pos16 < NINE, part, 0.0)
                    for shift in (1, 2, 4, 8):
                        part = part + roll(part, -shift if sy == 0 else shift)
                    total[half] = total[half] + inner[half] * part
        k = lax.broadcasted_iota(jnp.int32, (rows.size, LANES), 0) + rows.start
        weight = jnp.exp(0.1 * k.astype(F32)) * (3.0 / raw_sum)
        out = []
        for scale in (None, rate_ref):
            for value in (zonal, merid):
                for half in range(2):
                    by = weight if scale is None else rate_ref[rows, HALVES[half]]
                    out.append(by * value[half])
        return out

    totals = each_tile(fourth, tuple(jnp.zeros((8, LANES), F32) for _ in range(8)))
    values = [jnp.concatenate(totals[2 * i:2 * i + 2], axis=1) * (1.0 if i < 2 else 4.0 / FREQS) for i in range(4)]
    picked = slot8.astype(F32) == slot
    lanes_of = jnp.concatenate(
        [jnp.where(picked, v, 0.0) for v in values] + [jnp.zeros((LANES - 32, CELLS), F32)], axis=0)
    back_s[...] = dot(from_source[:, 0:CELLS], lanes_of, ((1,), (1,))).reshape(n_tile, 1, LANES)
    rows_wait(rows_s, send_sem)
    send_row(back_s, back_r, back_sem)

    rows_wait(back_r, back_sem)
    rows_wait(back_s, send_sem)
    for copy in x_copy + i_copy + y_copy + c_copy + f_copy:
        copy.wait_send()


def finish(n_tile, e_ref, back_ref, route_hbm, out_hbm, coup_ref, route_in, in_sem, out_sem):
    copy = pltpu.make_async_copy(route_hbm, route_in, in_sem.at[0])
    copy.start()
    result = [
        pltpu.make_async_copy(
            e_ref.at[pl.ds(NINE * q, NINE)], out_hbm.at[pl.ds(NINE * q, NINE)], out_sem.at[q])
        for q in range(4)
    ]
    for part in result:
        part.start()
    copy.wait()
    tiles = lax.broadcasted_iota(jnp.int32, (n_tile, CELLS), 0)
    slot8 = lax.broadcasted_iota(jnp.int32, (8, CELLS), 0)
    to_dest = jnp.where(tiles == route_in[0:1], 1.0, 0.0).astype(F32)
    found = dot(back_ref[...].reshape(n_tile, LANES).T, to_dest, ((1,), (0,)))
    for c in range(4):
        coup_ref[c:c + 1] = jnp.sum(
            jnp.where(slot8 == route_in[1:2], found[8 * c:8 * c + 8], 0.0), axis=0, keepdims=True)
    for part in result:
        part.wait()


def solution(mesh):
    n_grp, n_tile = mesh.shape["grp"], mesh.shape["tile"]

    def body(spectrum, courant, decay, land, ice_rows, ice_route, wave_source):
        vmem = pltpu.VMEM
        dma = pltpu.SemaphoreType.DMA
        scratch = [
            vmem((DIRS, FREQS, CELLS), F32),
            vmem((1, FREQS), F32), vmem((1, FREQS), F32), vmem((SIDE, SIDE), jnp.int32),
            vmem((3, CELLS), F32), vmem((2, CELLS), jnp.int32), vmem((2, SIDE, SIDE), jnp.int32),
            vmem((10, 8, LANES), F32),
            vmem((FREQS, LANES), F32), vmem((FREQS, LANES), F32),
            vmem((FREQS, CELLS), F32), vmem((FREQS, CELLS), F32),
            vmem((FREQS, CELLS), F32), vmem((FREQS, CELLS), F32),
            vmem((2, 6, FREQS, LANES), F32), vmem((2, 6, FREQS, LANES), F32),
            vmem((2, 8, LANES), F32), vmem((2, 8, LANES), F32),
            vmem((2, 4, FREQS, CELLS), F32), vmem((2, 4, FREQS, CELLS), F32),
            vmem((4, 3, FREQS, LANES), F32), vmem((4, 3, FREQS, LANES), F32),
            vmem((2, 8, CELLS), F32), vmem((2, 8, CELLS), F32),
            vmem((n_tile, 1, LANES), F32), vmem((n_tile, 1, LANES), F32), vmem((n_tile, 1, LANES), F32),
            dma((6,)), dma((4,)), dma((13,)), dma((2,)), dma((2,)), dma((2,)), dma((4,)), dma((2,)),
            dma((1,)), dma((1,)),
        ]
        anywhere = pl.BlockSpec(memory_space=pl.ANY)
        held = pl.BlockSpec(memory_space=pltpu.VMEM)
        energy, back = pl.pallas_call(
            functools.partial(kernel, n_grp, n_tile),
            out_shape=(pltpu.VMEM((DIRS, FREQS, CELLS), F32), pltpu.VMEM((n_tile, 1, LANES), F32)),
            in_specs=[anywhere] * 7,
            out_specs=(held, held),
            scratch_shapes=scratch,
            name="coupling_step",
            compiler_params=pltpu.CompilerParams(
                collective_id=0, has_side_effects=True, vmem_limit_bytes=60 * 1024 * 1024),
        )(spectrum, courant.reshape(1, FREQS), decay.reshape(1, FREQS), land, ice_rows, ice_route, wave_source)
        return pl.pallas_call(
            functools.partial(finish, n_tile),
            out_shape=(
                jax.ShapeDtypeStruct((DIRS, FREQS, CELLS), F32),
                jax.ShapeDtypeStruct((4, CELLS), F32),
            ),
            in_specs=[held, held, anywhere],
            out_specs=(anywhere, held),
            scratch_shapes=[vmem((2, CELLS), jnp.int32), dma((1,)), dma((4,))],
            name="coupling_finish",
            compiler_params=pltpu.CompilerParams(vmem_limit_bytes=8 * 1024 * 1024),
        )(energy, back, ice_route)

    in_specs = (
        P(None, None, ("grp", "tile")),
        P(),
        P(),
        P("tile", "grp"),
        P(None, ("grp", "tile")),
        P(None, ("grp", "tile")),
        P(None, "tile", "grp"),
    )
    out_specs = (P(None, None, ("grp", "tile")), P(None, ("grp", "tile")))
    return jax.shard_map(body, mesh=mesh, in_specs=in_specs, out_specs=out_specs, check_vma=False)
```

time: 53.7 us -> 43.7 us (0.81)
  Pallas kernels: 49.7 us -> 42.9 us
  local copies, waits for them, and re-layouts: 3.18 us -> 0.01 us
    pallas_call x1 -> x2, Pallas kernels: 49.7 us -> 42.9 us  [the longest x1 41.2 us: body(): pl.pallas_call(functools.partial(kernel, n_grp, n_tile), out_shape=(pltpu...]
    unnamed x4 -> x2, local copies, waits for them, and re-layouts: 3.18 us -> 0.01 us
where the time goes in v2:
time: 43.7 us; the launch traced here: 43.6 us
  Pallas kernels  42.9 us (98%)
  between operations  0.66 us (2%)
    pallas_call x1, Pallas kernels, body(): pl.pallas_call(functools.partial(kernel, n_grp, n_tile), out_shape=(pltpu...  41.2 us
    pallas_call x1, Pallas kernels, body(): pl.pallas_call(functools.partial(finish, n_tile), out_shape=(jax.ShapeDty...  1.74 us

profile of v2, /device:TPU:1, one launch (start us, length us, event | category | flops | bytes accessed | tf_op | source)
XLA Modules:
  0.0 43.6 jit_solution(2203609166971756314)
XLA Ops:
  0.6 0.0 copy-start
  0.6 41.2 %coupling_step.1 = (f32[36,36,256]{2,1,0:T(8,128)S(1)}, f32[64,1,128]{2,1,0:T(1,128)S(1)}) custom-call(f32[36,36,256]{2,1,0:T(8,128)} %spec_hbm.1, f32[1,36]{1,0:T(1,128)} %bitcast.2, f32[1,36]{1,0:T(1,128)} %bitcast.3, s32[16,16]{1,0:T(8,128)} %land_hbm.1, f32[3,256]{1,0:T(4,128)} %ice_hbm.1, s32[2,256]{1,0:T(2,128)} %route_hbm.3, s32[2,16,16]{2,1,0:T(8,128)} %source_hbm.1), custom_call_target="tpu_custom_call" | custom-call | tf_op jit(solution)/shard_map/coupling_step/pallas_call | solution.py:485
  41.8 0.0 copy-done
  41.9 1.7 %coupling_finish.1 = (f32[36,36,256]{2,1,0:T(8,128)}, f32[4,256]{1,0:T(4,128)}) custom-call(f32[36,36,256]{2,1,0:T(8,128)S(1)} %get-tuple-element.4.e_ref, f32[64,1,128]{2,1,0:T(1,128)S(1)} %get-tuple-element.5.back_ref, s32[2,256]{1,0:T(2,128)S(1)} %copy-done), custom_call_target="tpu_custom_call" | custom-call | tf_op jit(solution)/shard_map/coupling_finish/pallas_call | solution.py:495
Async XLA Ops:
  0.6 41.2 %copy-start = (s32[2,256]{1,0:T(2,128)S(1)}, s32[2,256]{1,0:T(2,128)}, u32[]{:S(2)}) copy-start(s32[2,256]{1,0:T(2,128)} %route_hbm.3) | copy-start | bytes 6148

commit v3 on v2

--- a/solution.py
+++ b/solution.py
@@ -30,6 +30,20 @@
 
 def dot(a, b, dims):
     return lax.dot_general(a, b, (dims, ((), ())), precision=lax.Precision.HIGHEST, preferred_element_type=F32)
+
+
+def split(value):
+    high = value.astype(jnp.bfloat16)
+    rest = value - high.astype(F32)
+    middle = rest.astype(jnp.bfloat16)
+    low = (rest - middle.astype(F32)).astype(jnp.bfloat16)
+    return jnp.concatenate([high, middle, low], axis=0)
+
+
+def gather(table, one_hot, rows):
+    found = lax.dot_general(
+        split(table.T[0:rows]), one_hot, (((1,), (0,)), ((), ())), preferred_element_type=F32)
+    return found[0:rows] + found[rows:2 * rows] + found[2 * rows:]
 
 
 def roll(value, shift):
@@ -255,7 +269,35 @@
         copy.wait_recv()
     sources = jnp.concatenate([source, xinfo_r[0, 0:1], xinfo_r[1, 0:1]], axis=1)
     wide = lax.broadcasted_iota(jnp.int32, (n_tile, CELLS + 2 * LANES), 0).astype(F32)
-    from_source = jnp.where(wide == sources, 1.0, 0.0).astype(F32)
+    from_source = jnp.where(wide == sources, 1.0, 0.0).astype(jnp.bfloat16)
+
+    rows_wait(rows_r, rows_sem)
+    found = gather(rows_r[...].reshape(n_tile, LANES), from_source, 96)
+
+    def pick(section, cut, slots):
+        width = slots.shape[1]
+        mask = lax.broadcasted_iota(jnp.int32, (8, width), 0).astype(F32) == slots
+        return [
+            jnp.sum(jnp.where(mask, found[32 * section + 8 * c:32 * section + 8 * c + 8, cut], 0.0), axis=0, keepdims=True)
+            for c in range(3)
+        ]
+
+    field = pick(1, slice(0, CELLS), slot)
+    near = [
+        pick(2 * s, slice(CELLS + LANES * s, CELLS + LANES * (s + 1)), xinfo_r[s, 1:2]) for s in range(2)
+    ]
+
+    fields = jnp.concatenate(field + [land, jnp.zeros((4, CELLS), F32)], axis=0)
+    for s in range(2):
+        for part in range(2):
+            cut = slice(LANES * part, LANES * (part + 1))
+            edge = jnp.where(pos16 == (SIDE - 1 if s == 0 else 0), fields[:, cut], 0.0)
+            for shift in (1, 2, 4, 8):
+                edge = edge + roll(edge, -shift if s == 0 else shift)
+            yf_s[s, :, cut] = edge
+    f_copy = [remote(yf_s.at[s], yf_r.at[s], send_sem.at[11 + s], yf_sem.at[s], y_to[s]) for s in range(2)]
+    for copy in f_copy:
+        copy.start()
 
     for copy in x_copy + y_copy + c_copy:
         copy.wait_recv()
@@ -296,35 +338,6 @@
         return ()
 
     each_tile(second)
-
-    rows_wait(rows_r, rows_sem)
-    arrived = rows_r[...].reshape(n_tile, LANES).T
-    found = dot(arrived, from_source, ((1,), (0,)))
-
-    def pick(section, cut, slots):
-        width = slots.shape[1]
-        mask = lax.broadcasted_iota(jnp.int32, (8, width), 0).astype(F32) == slots
-        return [
-            jnp.sum(jnp.where(mask, found[32 * section + 8 * c:32 * section + 8 * c + 8, cut], 0.0), axis=0, keepdims=True)
-            for c in range(3)
-        ]
-
-    field = pick(1, slice(0, CELLS), slot)
-    near = [
-        pick(2 * s, slice(CELLS + LANES * s, CELLS + LANES * (s + 1)), xinfo_r[s, 1:2]) for s in range(2)
-    ]
-
-    fields = jnp.concatenate(field + [land, jnp.zeros((4, CELLS), F32)], axis=0)
-    for s in range(2):
-        for part in range(2):
-            cut = slice(LANES * part, LANES * (part + 1))
-            edge = jnp.where(pos16 == (SIDE - 1 if s == 0 else 0), fields[:, cut], 0.0)
-            for shift in (1, 2, 4, 8):
-                edge = edge + roll(edge, -shift if s == 0 else shift)
-            yf_s[s, :, cut] = edge
-    f_copy = [remote(yf_s.at[s], yf_r.at[s], send_sem.at[11 + s], yf_sem.at[s], y_to[s]) for s in range(2)]
-    for copy in f_copy:
-        copy.start()
 
     def rate_of(rows, values):
         conc, thick, floe = values
@@ -392,12 +405,8 @@
                 cut = HALVES[half]
                 rim = yf_r[sy, 3:4, cut] * jnp.exp(-rate_of(rows, [yf_r[sy, c:c + 1, cut] for c in range(3)]))
                 message[half] = [yr[sy, 2 + arr, rows, cut] * rim for arr in range(2)]
-            for q in (2 * sy, 2 * sy + 1):
-                for j in range(NINE):
-                    d = NINE * q + j
-                    for half in range(2):
-                        cut = HALVES[half]
-                        e0[d, rows, cut] = e0[d, rows, cut] + inner[half] * halo_y(q, j, message[half][q % 2])
+                for arr in range(2):
+                    yr[sy, 2 + arr, rows, cut] = message[half][arr]
             for half in range(2):
                 pair = message[half]
                 sign = [1.0 if QUADS[2 * sy + arr][0] == 0 else -1.0 for arr in range(2)]
@@ -423,12 +432,29 @@
     totals = each_tile(fourth, tuple(jnp.zeros((8, LANES), F32) for _ in range(8)))
     values = [jnp.concatenate(totals[2 * i:2 * i + 2], axis=1) * (1.0 if i < 2 else 4.0 / FREQS) for i in range(4)]
     picked = slot8.astype(F32) == slot
-    lanes_of = jnp.concatenate(
-        [jnp.where(picked, v, 0.0) for v in values] + [jnp.zeros((LANES - 32, CELLS), F32)], axis=0)
-    back_s[...] = dot(from_source[:, 0:CELLS], lanes_of, ((1,), (1,))).reshape(n_tile, 1, LANES)
+    lanes_of = split(jnp.concatenate([jnp.where(picked, v, 0.0) for v in values], axis=0))
+    lanes_of = jnp.concatenate([lanes_of, jnp.zeros((LANES - 96, CELLS), jnp.bfloat16)], axis=0)
+    table = lax.dot_general(
+        from_source[:, 0:CELLS], lanes_of, (((1,), (1,)), ((), ())), preferred_element_type=F32)
+    table = table + roll(table, -32) + roll(table, -64)
+    back_s[...] = table.reshape(n_tile, 1, LANES)
     rows_wait(rows_s, send_sem)
     send_row(back_s, back_r, back_sem)
 
+    def fifth(rows):
+        _, _, _, _, first_y = masks(rows.size)
+        for sy in range(2):
+            for half in range(2):
+                cut = HALVES[half]
+                inner = jnp.where(first_y[sy], factor_ref[rows, cut], 0.0)
+                for q in (2 * sy, 2 * sy + 1):
+                    message = yr[sy, 2 + q % 2, rows, cut]
+                    for j in range(NINE):
+                        d = NINE * q + j
+                        e0[d, rows, cut] = e0[d, rows, cut] + inner * halo_y(q, j, message)
+        return ()
+
+    each_tile(fifth)
     rows_wait(back_r, back_sem)
     rows_wait(back_s, send_sem)
     for copy in x_copy + i_copy + y_copy + c_copy + f_copy:
@@ -448,8 +474,8 @@
     copy.wait()
     tiles = lax.broadcasted_iota(jnp.int32, (n_tile, CELLS), 0)
     slot8 = lax.broadcasted_iota(jnp.int32, (8, CELLS), 0)
-    to_dest = jnp.where(tiles == route_in[0:1], 1.0, 0.0).astype(F32)
-    found = dot(back_ref[...].reshape(n_tile, LANES).T, to_dest, ((1,), (0,)))
+    to_dest = jnp.where(tiles == route_in[0:1], 1.0, 0.0).astype(jnp.bfloat16)
+    found = gather(back_ref[...].reshape(n_tile, LANES), to_dest, 32)
     for c in range(4):
         coup_ref[c:c + 1] = jnp.sum(
             jnp.where(slot8 == route_in[1:2], found[8 * c:8 * c + 8], 0.0), axis=0, keepdims=True)

time: 43.7 us -> 42.5 us (0.973)
  Pallas kernels: 42.9 us -> 41.7 us
    pallas_call x1, Pallas kernels: 41.2 us -> 40 us  [body(): pl.pallas_call(functools.partial(kernel, n_grp, n_tile), out_shape=(pltpu...]
where the time goes in v3:
time: 42.5 us; the launch traced here: 42.4 us
  Pallas kernels  41.7 us (98%)
  between operations  0.66 us (2%)
    pallas_call x1, Pallas kernels, body(): pl.pallas_call(functools.partial(kernel, n_grp, n_tile), out_shape=(pltpu...  40 us
    pallas_call x1, Pallas kernels, body(): pl.pallas_call(functools.partial(finish, n_tile), out_shape=(jax.ShapeDty...  1.74 us

profile of v3, /device:TPU:1, one launch (start us, length us, event | category | flops | bytes accessed | tf_op | source)
XLA Modules:
  0.0 42.4 jit_solution(397950736023888543)
XLA Ops:
  0.6 0.0 copy-start
  0.6 40.0 %coupling_step.1 = (f32[36,36,256]{2,1,0:T(8,128)S(1)}, f32[64,1,128]{2,1,0:T(1,128)S(1)}) custom-call(f32[36,36,256]{2,1,0:T(8,128)} %spec_hbm.1, f32[1,36]{1,0:T(1,128)} %bitcast.2, f32[1,36]{1,0:T(1,128)} %bitcast.3, s32[16,16]{1,0:T(8,128)} %land_hbm.1, f32[3,256]{1,0:T(4,128)} %ice_hbm.1, s32[2,256]{1,0:T(2,128)} %route_hbm.3, s32[2,16,16]{2,1,0:T(8,128)} %source_hbm.1), custom_call_target="tpu_custom_call" | custom-call | tf_op jit(solution)/shard_map/coupling_step/pallas_call | solution.py:511
  40.6 0.0 copy-done
  40.7 1.7 %coupling_finish.1 = (f32[36,36,256]{2,1,0:T(8,128)}, f32[4,256]{1,0:T(4,128)}) custom-call(f32[36,36,256]{2,1,0:T(8,128)S(1)} %get-tuple-element.4.e_ref, f32[64,1,128]{2,1,0:T(1,128)S(1)} %get-tuple-element.5.back_ref, s32[2,256]{1,0:T(2,128)S(1)} %copy-done), custom_call_target="tpu_custom_call" | custom-call | tf_op jit(solution)/shard_map/coupling_finish/pallas_call | solution.py:521
Async XLA Ops:
  0.6 40.0 %copy-start = (s32[2,256]{1,0:T(2,128)S(1)}, s32[2,256]{1,0:T(2,128)}, u32[]{:S(2)}) copy-start(s32[2,256]{1,0:T(2,128)} %route_hbm.3) | copy-start | bytes 6148

commit v4 on v3

--- a/solution.py
+++ b/solution.py
@@ -394,7 +394,7 @@
 
     def fourth(rows):
         _, _, pos16, _, first_y = masks(rows.size)
-        weight_of = [weights[6 + i, 0:rows.size] for i in range(4)]
+        weight_of = [weights[6 + i, 0:1] for i in range(4)]
         factor = [factor_ref[rows, cut] for cut in HALVES]
         zonal = [zonal_ref[rows, cut] for cut in HALVES]
         merid = [merid_ref[rows, cut] for cut in HALVES]
@@ -429,7 +429,7 @@
                     out.append(by * value[half])
         return out
 
-    totals = each_tile(fourth, tuple(jnp.zeros((8, LANES), F32) for _ in range(8)))
+    totals = [jnp.sum(v, axis=0, keepdims=True) for v in fourth(pl.ds(0, FREQS))]
     values = [jnp.concatenate(totals[2 * i:2 * i + 2], axis=1) * (1.0 if i < 2 else 4.0 / FREQS) for i in range(4)]
     picked = slot8.astype(F32) == slot
     lanes_of = split(jnp.concatenate([jnp.where(picked, v, 0.0) for v in values], axis=0))

time: 42.5 us -> 41.3 us (0.972)
  Pallas kernels: 41.7 us -> 40.5 us
    pallas_call x1, Pallas kernels: 40 us -> 38.8 us  [body(): pl.pallas_call(functools.partial(kernel, n_grp, n_tile), out_shape=(pltpu...]
where the time goes in v4:
time: 41.3 us; the launch traced here: 41.2 us
  Pallas kernels  40.5 us (98%)
  between operations  0.66 us (2%)
    pallas_call x1, Pallas kernels, body(): pl.pallas_call(functools.partial(kernel, n_grp, n_tile), out_shape=(pltpu...  38.8 us
    pallas_call x1, Pallas kernels, body(): pl.pallas_call(functools.partial(finish, n_tile), out_shape=(jax.ShapeDty...  1.74 us

profile of v4, /device:TPU:1, one launch (start us, length us, event | category | flops | bytes accessed | tf_op | source)
XLA Modules:
  0.0 41.2 jit_solution(4733962960887635173)
XLA Ops:
  0.6 0.0 copy-start
  0.6 38.8 %coupling_step.1 = (f32[36,36,256]{2,1,0:T(8,128)S(1)}, f32[64,1,128]{2,1,0:T(1,128)S(1)}) custom-call(f32[36,36,256]{2,1,0:T(8,128)} %spec_hbm.1, f32[1,36]{1,0:T(1,128)} %bitcast.2, f32[1,36]{1,0:T(1,128)} %bitcast.3, s32[16,16]{1,0:T(8,128)} %land_hbm.1, f32[3,256]{1,0:T(4,128)} %ice_hbm.1, s32[2,256]{1,0:T(2,128)} %route_hbm.3, s32[2,16,16]{2,1,0:T(8,128)} %source_hbm.1), custom_call_target="tpu_custom_call" | custom-call | tf_op jit(solution)/shard_map/coupling_step/pallas_call | solution.py:511
  39.5 0.0 copy-done
  39.5 1.7 %coupling_finish.1 = (f32[36,36,256]{2,1,0:T(8,128)}, f32[4,256]{1,0:T(4,128)}) custom-call(f32[36,36,256]{2,1,0:T(8,128)S(1)} %get-tuple-element.4.e_ref, f32[64,1,128]{2,1,0:T(1,128)S(1)} %get-tuple-element.5.back_ref, s32[2,256]{1,0:T(2,128)S(1)} %copy-done), custom_call_target="tpu_custom_call" | custom-call | tf_op jit(solution)/shard_map/coupling_finish/pallas_call | solution.py:521
Async XLA Ops:
  0.6 38.8 %copy-start = (s32[2,256]{1,0:T(2,128)S(1)}, s32[2,256]{1,0:T(2,128)}, u32[]{:S(2)}) copy-start(s32[2,256]{1,0:T(2,128)} %route_hbm.3) | copy-start | bytes 6148

commit v5 on v4

--- a/solution.py
+++ b/solution.py
@@ -305,8 +305,8 @@
     def second(rows):
         _, slot16, pos16, first_x, first_y = masks(rows.size)
         cour = cour_ref[rows]
-        x_weight = [cour * weights[i, 0:rows.size] for i in range(6)]
-        y_weight = [cour * weights[6 + i, 0:rows.size] for i in range(4)]
+        x_weight = [cour * weights[i, 0:1] for i in range(6)]
+        y_weight = [cour * weights[6 + i, 0:1] for i in range(4)]
         for q in range(4):
             sx, sy = QUADS[q]
             x_edge = [x_weight[n] * (xr[sx, n, rows] * edge_x[sx]) for n in range(3)]
@@ -337,7 +337,7 @@
                 yr[sy, 2 + q % 2, rows, HALVES[half]] = whole * (y_weight[2 + q % 2] * edge_y[sy])
         return ()
 
-    each_tile(second)
+    second(pl.ds(0, FREQS))
 
     def rate_of(rows, values):
         conc, thick, floe = values

time: 41.3 us -> 41.1 us (level)
  no operation moved by 1% of the time
where the time goes in v5:
time: 41.1 us; the launch traced here: 40.9 us
  Pallas kernels  40.3 us (98%)
  between operations  0.66 us (2%)
    pallas_call x1, Pallas kernels, body(): pl.pallas_call(functools.partial(kernel, n_grp, n_tile), out_shape=(pltpu...  38.5 us
    pallas_call x1, Pallas kernels, body(): pl.pallas_call(functools.partial(finish, n_tile), out_shape=(jax.ShapeDty...  1.74 us

profile of v5, /device:TPU:1, one launch (start us, length us, event | category | flops | bytes accessed | tf_op | source)
XLA Modules:
  0.0 40.9 jit_solution(13739899396794034914)
XLA Ops:
  0.6 0.0 copy-start
  0.6 38.5 %coupling_step.1 = (f32[36,36,256]{2,1,0:T(8,128)S(1)}, f32[64,1,128]{2,1,0:T(1,128)S(1)}) custom-call(f32[36,36,256]{2,1,0:T(8,128)} %spec_hbm.1, f32[1,36]{1,0:T(1,128)} %bitcast.2, f32[1,36]{1,0:T(1,128)} %bitcast.3, s32[16,16]{1,0:T(8,128)} %land_hbm.1, f32[3,256]{1,0:T(4,128)} %ice_hbm.1, s32[2,256]{1,0:T(2,128)} %route_hbm.3, s32[2,16,16]{2,1,0:T(8,128)} %source_hbm.1), custom_call_target="tpu_custom_call" | custom-call | tf_op jit(solution)/shard_map/coupling_step/pallas_call | solution.py:511
  39.2 0.0 copy-done
  39.2 1.7 %coupling_finish.1 = (f32[36,36,256]{2,1,0:T(8,128)}, f32[4,256]{1,0:T(4,128)}) custom-call(f32[36,36,256]{2,1,0:T(8,128)S(1)} %get-tuple-element.4.e_ref, f32[64,1,128]{2,1,0:T(1,128)S(1)} %get-tuple-element.5.back_ref, s32[2,256]{1,0:T(2,128)S(1)} %copy-done), custom_call_target="tpu_custom_call" | custom-call | tf_op jit(solution)/shard_map/coupling_finish/pallas_call | solution.py:521
Async XLA Ops:
  0.6 38.5 %copy-start = (s32[2,256]{1,0:T(2,128)S(1)}, s32[2,256]{1,0:T(2,128)}, u32[]{:S(2)}) copy-start(s32[2,256]{1,0:T(2,128)} %route_hbm.3) | copy-start | bytes 6148
